TPU v7x, 32 devices: a whole 2x2x4 slice. The times are simulated.
32 devices in a mesh: req: 8 (over y, x, core), tp: 4 (over z).
Axes of the slice: x: 2, y: 2, z: 4, core: 2. Of those that a mesh axis runs over, the one named last changes fastest.
Arguments:
- hidden: bfloat16 [8, 8192], P(None, 'req')
- attn_gain: bfloat16 [2, 8192], P(None, 'req'), may hold values from 0.5 to 1.5
- q_weight: bfloat16 [2, 8192, 4096], P(None, 'req', 'tp'), may hold values from -0.0625 to 0.0625
- o_weight: bfloat16 [2, 4096, 8192], P(None, 'tp', 'req'), may hold values from -0.09375 to 0.09375
- ffn_gain: bfloat16 [2, 8192], P(None, 'req'), may hold values from 0.5 to 1.5
- gate_weight: bfloat16 [2, 8192, 14336], P(None, 'req', 'tp'), may hold values from -0.0625 to 0.0625
- up_weight: bfloat16 [2, 8192, 14336], P(None, 'req', 'tp'), may hold values from -0.0625 to 0.0625
- down_weight: bfloat16 [2, 14336, 8192], P(None, 'tp', 'req'), may hold values from -0.046875 to 0.046875
- kv_pool: bfloat16 [2, 256, 4, 2, 128, 128], P(None, 'req', 'tp')
- block_home: int32 [8, 32], P('req'), may hold values from 0 to 255, as said below
- chosen: int32 [2, 8, 4, 24], P(None, 'req', 'tp'), may hold values from 0 to 31, as said below
- chosen_count: int32 [2, 8, 4], P(None, 'req', 'tp'), may hold values from 6 to 24
Outputs:
- new_hidden: bfloat16 [8, 8192], P(None, 'req')
Inputs may be any that keep to these rules, and one draw needn't show every extreme that they name: `block_home`: pool slot p lies on store device p // 32 of req; every slot belongs to exactly one block of one request, and every request has exactly 4 blocks on each store device. `chosen`: entries of a list are distinct. The used entries of a list are all 4 blocks of some store devices and some blocks of one more; entries from chosen_count on are ignored.
All inputs are finite; a program needn't handle non-finite values.
Results may differ from a plain program's by a relative error of at most 0.038.
Values may be sent and summed in bfloat16 or wider, within the bound.
A program may use at most 128 MiB of HBM per device.

v0:
```python
import math

import jax
import jax.numpy as jnp
from jax import lax
from jax.sharding import PartitionSpec as P

D = 8192
LAYERS = 2


MASK_FILL = -1e30
EPSILON = 1e-05


def rotary(queries, position):
    head_size = queries.shape[-1]
    half_size = head_size // 2
    freq_idx = jnp.arange(half_size).astype(queries.dtype)
    angles = position * jnp.exp(freq_idx * (-2.0 * math.log(500000.0) / head_size))
    cosine = jnp.cos(angles)
    sine_part = jnp.sin(angles)
    lower_half = queries[..., :half_size]
    upper_half = queries[..., half_size:]
    return jnp.concatenate(
        [
            lower_half * cosine - upper_half * sine_part,
            upper_half * cosine + lower_half * sine_part,
        ],
        axis=-1,
    )


def local_squares(current):
    widened = current.astype(jnp.float32)
    return jnp.sum(widened * widened, axis=1)


def apply_gain(current, gain):
    return (current.astype(jnp.float32) * gain.astype(jnp.float32)).astype(jnp.bfloat16)


def inverse_of(squares):
    return lax.rsqrt(squares / D + EPSILON)


def summed_inverse(current):
    return inverse_of(lax.psum(local_squares(current), "req"))


def sum_over_heads(partial_sum):
    return lax.psum(partial_sum, "tp")


def block_stats(queries, blocks, valid):
    scores = jnp.einsum(
        "sigeh,sigqbh->sigeqb", queries, blocks[:, :, :, :, 0], preferred_element_type=jnp.float32
    )
    block_max = jnp.max(scores, axis=5)
    exp_terms = jnp.exp(scores - block_max[..., None])
    block_sum = jnp.sum(exp_terms, axis=5)
    block_acc = jnp.einsum(
        "sigeqb,sigqbh->sigeqh",
        exp_terms.astype(jnp.bfloat16),
        blocks[:, :, :, :, 1],
        preferred_element_type=jnp.float32,
    )
    block_max = jnp.where(valid[:, :, :, None, :], block_max, MASK_FILL)
    return (block_max, block_sum, block_acc)


def combine(block_max, block_sum, block_acc, axes):
    overall = jnp.max(block_max, axis=axes, keepdims=True)
    rescale = jnp.exp(block_max - overall)
    numerator = jnp.sum(rescale[..., None] * block_acc, axis=axes)
    denominator = jnp.sum(rescale * block_sum, axis=axes)
    return (jnp.squeeze(overall, axes), denominator, numerator)


def shards(
    hidden,
    attn_gain,
    q_weight,
    o_weight,
    ffn_gain,
    gate_weight,
    up_weight,
    down_weight,
    kv_pool,
    block_home,
    chosen,
    chosen_count,
):
    n_req = lax.axis_size("req")
    req_dev = chosen.shape[1]
    heads_dev = chosen.shape[2]
    most_sel = chosen.shape[3]
    pool_dev = kv_pool.shape[1]
    head_size = kv_pool.shape[5]
    per_store = block_home.shape[1] // n_req
    position = float(block_home.shape[1] * kv_pool.shape[4] - 1)
    own_start = lax.axis_index("req") * req_dev
    row_index = jnp.arange(req_dev)[:, None, None]
    entries = jnp.arange(most_sel)
    store_ids = jnp.arange(n_req)[:, None, None, None, None]
    slot_ids = jnp.arange(per_store)[None, None, None, :, None]
    head_index = jnp.arange(heads_dev)[None, None, :, None]
    current = hidden
    for layer_no in range(LAYERS):
        scaled = apply_gain(current, attn_gain[layer_no])
        inv_all = summed_inverse(current)
        rows_in = scaled
        product = jnp.dot(rows_in, q_weight[layer_no], preferred_element_type=jnp.float32)
        summed = lax.psum_scatter(product, "req", scatter_dimension=0, tiled=True)
        inv_own = lax.dynamic_slice_in_dim(inv_all, own_start, req_dev, 0)
        queries = (summed * inv_own[:, None]).reshape(req_dev, heads_dev, -1, head_size)
        queries = (rotary(queries, position) * head_size ** (-0.5)).astype(jnp.bfloat16)
        pool_ids = block_home[row_index, chosen[layer_no]]
        home_store = pool_ids // pool_dev
        home_slot = pool_ids % pool_dev
        used_mask = entries[None, None, :] < chosen_count[layer_no][:, :, None]
        earlier = (
            (home_store[..., :, None] == home_store[..., None, :])
            & used_mask[..., None, :]
            & (entries[None, :] < entries[:, None])
        )
        rank = jnp.sum(earlier.astype(jnp.int32), axis=-1)
        match = (
            (home_store[None, :, :, None, :] == store_ids)
            & (rank[None, :, :, None, :] == slot_ids)
            & used_mask[None, :, :, None, :]
        )
        wanted = jnp.sum(jnp.where(match, home_slot[None, :, :, None, :] + 1, 0), axis=4) - 1
        received_ids = lax.all_to_all(wanted, "req", split_axis=0, concat_axis=0, tiled=True)
        served = kv_pool[layer_no][jnp.maximum(received_ids, 0), head_index]
        fetched = lax.all_to_all(served, "req", split_axis=0, concat_axis=0, tiled=True)
        spread = jnp.broadcast_to(queries[None], (n_req,) + queries.shape)
        stats = block_stats(spread, fetched, wanted >= 0)
        overall, denominator, numerator = combine(stats[0], stats[1], stats[2], (0, 4))
        context = (numerator / denominator[..., None]).astype(jnp.bfloat16).reshape(req_dev, -1)
        attn_part = jnp.dot(
            lax.all_gather(context, "req", axis=0, tiled=True),
            o_weight[layer_no],
            preferred_element_type=jnp.float32,
        )
        attended = (current.astype(jnp.float32) + sum_over_heads(attn_part)).astype(jnp.bfloat16)
        scaled = apply_gain(attended, ffn_gain[layer_no])
        inv_all = summed_inverse(attended)
        gate = jnp.dot(scaled, gate_weight[layer_no], preferred_element_type=jnp.float32)
        up_part = jnp.dot(scaled, up_weight[layer_no], preferred_element_type=jnp.float32)
        payload = (gate, up_part)
        totals = lax.psum((payload[0], payload[1]), "req")
        gate = totals[0] * inv_all[:, None]
        up_part = totals[1] * inv_all[:, None]
        activated = (jax.nn.silu(gate) * up_part).astype(jnp.bfloat16)
        ffn_part = jnp.dot(activated, down_weight[layer_no], preferred_element_type=jnp.float32)
        current = (attended.astype(jnp.float32) + sum_over_heads(ffn_part)).astype(jnp.bfloat16)
    return current


def solution(mesh):
    return jax.shard_map(
        shards,
        mesh=mesh,
        in_specs=(
            P(None, "req"),
            P(None, "req"),
            P(None, "req", "tp"),
            P(None, "tp", "req"),
            P(None, "req"),
            P(None, "req", "tp"),
            P(None, "req", "tp"),
            P(None, "tp", "req"),
            P(None, "req", "tp", None, None, None),
            P("req", None),
            P(None, "req", "tp", None),
            P(None, "req", "tp"),
        ),
        out_specs=P(None, "req"),
        check_vma=False,
    )
```

profile of v0, /device:TPU:0, one launch (start us, length us, event | category | flops | bytes accessed | tf_op | source)
XLA Modules:
  0.0 394.2 jit_solution(4232964003404034233)
XLA Ops:
  11.1 5.2 %all-to-all-start = ((s32[8,1,1,4]{3,2,1,0:T(1,128)}), s32[8,1,1,4]{3,2,1,0:T(1,128)S(1)}, u32[]{:S(2)}, u32[]{:S(2)}) async-start(s32[8,1,1,4]{3,2,1,0:T(1,128)} %copy.66), calls=%async_computation | async-start | bytes 8192 | tf_op jit(solution)/shard_map/all_to_all | solution.py:134
  18.2 4.8 %slice_bitcast_fusion.1 = (bf16[32,1,2,128,128]{4,3,2,0,1:T(8,128)(2,1)}, bf16[32,1,2,128,128]{4,3,2,0,1:T(8,128)(2,1)}) fusion(bf16[2,32,1,2,128,128]{5,4,3,2,1,0:T(8,128)(2,1)} %param.20), kind=kLoop, calls=%fused_computation.34 | loop fusion | bytes 8388608 | tf_op jit(solution)/shard_map/squeeze | solution.py:135
  24.6 4.2 %all-to-all-start.2 = ((s32[8,1,1,4]{3,2,1,0:T(1,128)}), s32[8,1,1,4]{3,2,1,0:T(1,128)S(1)}, u32[]{:S(2)}, u32[]{:S(2)}) async-start(s32[8,1,1,4]{3,2,1,0:T(1,128)} %copy.73), calls=%async_computation.2 | async-start | bytes 8192 | tf_op jit(solution)/shard_map/all_to_all | solution.py:134
  33.4 4.4 %all-to-all-start.1 = ((bf16[8,1,1,4,2,128,128]{6,5,3,4,2,1,0:T(8,128)(2,1)}), bf16[8,1,1,4,2,128,128]{6,5,3,4,2,1,0:T(8,128)(2,1)}, u32[]{:S(2)}, u32[]{:S(2)}) async-start(bf16[8,1,1,4,2,128,128]{6,5,3,4,2,1,0:T(8,128)(2,1)} %copy.69), calls=%async_computation.1 | async-start | bytes 4194304 | tf_op jit(solution)/shard_map/all_to_all | solution.py:136
  39.7 41.8 %all-reduce.7 = (f32[8,1024]{1,0:T(8,128)S(1)}, f32[8]{0:T(128)S(1)}) all-reduce(f32[8,1024]{1,0:T(8,128)S(1)} %fusion.24, f32[8]{0:T(128)S(1)} %fusion.49), channel_id=2, replica_groups=mesh['req'=8,'tp'=4] {'req'}, use_global_device_ids=true, to_apply=%region_2.0.clone | all-reduce | flops 8200 | bytes 65600
  83.8 2.5 gather_fusion.3
  87.9 3.6 all-to-all-start.3
  95.4 25.8 %all-gather = bf16[8,1,1024]{2,1,0:T(2,128)(2,1)S(1)} all-gather(bf16[1,1,1024]{2,1,0:T(2,128)(2,1)S(1)} %convert_bitcast_fusion.1), channel_id=1, replica_groups=mesh['req'=8,'tp'=4] {'req'}, dimensions={0}, use_global_device_ids=true | all-gather | bytes 18432 | tf_op jit(solution)/shard_map/all_gather | solution.py:142
  123.2 19.2 %psum.85 = f32[8,1024]{1,0:T(8,128)S(1)} all-reduce(f32[8,1024]{1,0:T(8,128)S(1)} %fusion.22), channel_id=1, replica_groups=mesh['req'=8,'tp'=4] {'tp'}, use_global_device_ids=true, to_apply=%region_10.11 | all-reduce | flops 8192 | bytes 65536 | tf_op jit(solution)/shard_map/psum | solution.py:52
  142.6 4.8 %fusion.8 = f32[8,3584]{1,0:T(8,128)} fusion(bf16[2,1024,3584]{2,1,0:T(8,128)(2,1)} %param.18, bf16[8,1024]{1,0:T(8,128)(2,1)S(1)} %get-tuple-element.20, f32[1024]{0:T(1024)S(1)} %bitcast.151), kind=kOutput, calls=%fused_computation.12 | convolution fusion | flops 58744832 | bytes 7475200 | tf_op jit(solution)/shard_map/dot_general | solution.py:150
  147.4 4.8 %fusion.10 = f32[8,3584]{1,0:T(8,128)} fusion(bf16[2,1024,3584]{2,1,0:T(8,128)(2,1)} %param.17, bf16[8,1024]{1,0:T(8,128)(2,1)S(1)} %get-tuple-element.20, f32[1024]{0:T(1024)S(1)} %bitcast.152), kind=kOutput, calls=%fused_computation.14 | convolution fusion | flops 58744832 | bytes 7475200 | tf_op jit(solution)/shard_map/dot_general | solution.py:149
  152.2 11.8 %psum.87 = f32[8]{0:T(128)S(1)} all-reduce(f32[8]{0:T(128)S(1)} %get-tuple-element.19), channel_id=1, replica_groups=mesh['req'=8,'tp'=4] {'req'}, use_global_device_ids=true, to_apply=%region_13.14 | all-reduce | flops 8 | bytes 64 | tf_op jit(solution)/shard_map/psum | solution.py:48
  164.0 48.7 %all-reduce.15.cloned.1.call-done = (f32[8,3584]{1,0:T(8,128)}, f32[8,3584]{1,0:T(8,128)}) async-done(((f32[8,3584]{1,0:T(8,128)}, f32[8,3584]{1,0:T(8,128)}), (f32[8,3584]{1,0:T(8,128)}, f32[8,3584]{1,0:T(8,128)})) %all-reduce.15.cloned.1.call-update) | async-done | bytes 229392 | tf_op jit(solution)/shard_map/psum | solution.py:152
  212.7 4.3 %fusion.6 = f32[8,1024]{1,0:T(8,128)S(1)} fusion(bf16[2,3584,1024]{2,1,0:T(8,128)(2,1)} %param.19, f32[8,3584]{1,0:T(8,128)} %get-tuple-element.11, f32[8,3584]{1,0:T(8,128)} %get-tuple-element.12, f32[8]{0:T(128)S(1)} %add_rsqrt_fusion.2), kind=kOutput, calls=%fused_computation.10 | convolution fusion | flops 58949632 | bytes 7602208 | tf_op jit(solution)/shard_map/dot_general | solution.py:156
  217.1 19.0 %psum.89 = f32[8,1024]{1,0:T(8,128)S(1)} all-reduce(f32[8,1024]{1,0:T(8,128)S(1)} %fusion.6), channel_id=1, replica_groups=mesh['req'=8,'tp'=4] {'tp'}, use_global_device_ids=true, to_apply=%region_15.16 | all-reduce | flops 8192 | bytes 65536 | tf_op jit(solution)/shard_map/psum | solution.py:52
  238.1 22.7 %all-reduce.6 = (f32[8,1024]{1,0:T(8,128)S(1)}, f32[8]{0:T(128)S(1)}) all-reduce(f32[8,1024]{1,0:T(8,128)S(1)} %fusion.20, f32[8]{0:T(128)S(1)} %get-tuple-element.17), channel_id=3, replica_groups=mesh['req'=8,'tp'=4] {'req'}, use_global_device_ids=true, to_apply=%region_18.19.clone | all-reduce | flops 8200 | bytes 65600
  264.3 9.8 %all-gather.1 = bf16[8,1,1024]{2,1,0:T(2,128)(2,1)S(1)} all-gather(bf16[1,1,1024]{2,1,0:T(2,128)(2,1)S(1)} %convert_bitcast_fusion), channel_id=1, replica_groups=mesh['req'=8,'tp'=4] {'req'}, dimensions={0}, use_global_device_ids=true | all-gather | bytes 18432 | tf_op jit(solution)/shard_map/all_gather | solution.py:142
  276.0 16.0 %psum.91 = f32[8,1024]{1,0:T(8,128)S(1)} all-reduce(f32[8,1024]{1,0:T(8,128)S(1)} %fusion.18), channel_id=1, replica_groups=mesh['req'=8,'tp'=4] {'tp'}, use_global_device_ids=true, to_apply=%region_26.27 | all-reduce | flops 8192 | bytes 65536 | tf_op jit(solution)/shard_map/psum | solution.py:52
  292.2 4.8 %fusion.2 = f32[8,3584]{1,0:T(8,128)} fusion(bf16[2,1024,3584]{2,1,0:T(8,128)(2,1)} %param.18, bf16[8,1024]{1,0:T(8,128)(2,1)S(1)} %get-tuple-element.14, f32[1024]{0:T(1024)S(1)} %bitcast.149), kind=kOutput, calls=%fused_computation.6 | convolution fusion | flops 58744832 | bytes 7475200 | tf_op jit(solution)/shard_map/dot_general | solution.py:150
  297.0 4.8 %fusion.4 = f32[8,3584]{1,0:T(8,128)} fusion(bf16[2,1024,3584]{2,1,0:T(8,128)(2,1)} %param.17, bf16[8,1024]{1,0:T(8,128)(2,1)S(1)} %get-tuple-element.14, f32[1024]{0:T(1024)S(1)} %bitcast.150), kind=kOutput, calls=%fused_computation.8 | convolution fusion | flops 58744832 | bytes 7475200 | tf_op jit(solution)/shard_map/dot_general | solution.py:149
  301.8 11.8 %psum.93 = f32[8]{0:T(128)S(1)} all-reduce(f32[8]{0:T(128)S(1)} %get-tuple-element.13), channel_id=1, replica_groups=mesh['req'=8,'tp'=4] {'req'}, use_global_device_ids=true, to_apply=%region_29.30 | all-reduce | flops 8 | bytes 64 | tf_op jit(solution)/shard_map/psum | solution.py:48
  313.6 49.8 %all-reduce.13.cloned.1.call-done = (f32[8,3584]{1,0:T(8,128)}, f32[8,3584]{1,0:T(8,128)}) async-done(((f32[8,3584]{1,0:T(8,128)}, f32[8,3584]{1,0:T(8,128)}), (f32[8,3584]{1,0:T(8,128)}, f32[8,3584]{1,0:T(8,128)})) %all-reduce.13.cloned.1.call-update) | async-done | bytes 229392 | tf_op jit(solution)/shard_map/psum | solution.py:152
  363.4 4.3 %fusion = f32[8,1024]{1,0:T(8,128)S(1)} fusion(bf16[2,3584,1024]{2,1,0:T(8,128)(2,1)} %param.19, f32[8,3584]{1,0:T(8,128)} %get-tuple-element.9, f32[8,3584]{1,0:T(8,128)} %get-tuple-element.10, f32[8]{0:T(128)S(1)} %add_rsqrt_fusion), kind=kOutput, calls=%fused_computation.4 | convolution fusion | flops 58949632 | bytes 7602208 | tf_op jit(solution)/shard_map/dot_general | solution.py:156
  367.7 19.0 %psum.95 = f32[8,1024]{1,0:T(8,128)S(1)} all-reduce(f32[8,1024]{1,0:T(8,128)S(1)} %fusion), channel_id=1, replica_groups=mesh['req'=8,'tp'=4] {'tp'}, use_global_device_ids=true, to_apply=%region_31.32 | all-reduce | flops 8192 | bytes 65536 | tf_op jit(solution)/shard_map/psum | solution.py:52
  (101 shorter events, 32.7 us)
Async XLA Ops:
  6.5 2.1 copy-start
  11.1 13.5 %all-to-all-start = ((s32[8,1,1,4]{3,2,1,0:T(1,128)}), s32[8,1,1,4]{3,2,1,0:T(1,128)S(1)}, u32[]{:S(2)}, u32[]{:S(2)}) async-start(s32[8,1,1,4]{3,2,1,0:T(1,128)} %copy.66), calls=%async_computation | async-start | bytes 8192 | tf_op jit(solution)/shard_map/all_to_all | solution.py:134
  18.1 5.5 %copy-start.3 = (bf16[2,1024]{1,0:T(2,128)(2,1)S(1)}, bf16[2,1024]{1,0:T(2,128)(2,1)}, u32[]{:S(2)}) copy-start(bf16[2,1024]{1,0:T(2,128)(2,1)} %param.13) | copy-start | bytes 12292
  18.1 5.5 %copy-start.2 = (bf16[8,1024]{1,0:T(8,128)(2,1)S(1)}, bf16[8,1024]{1,0:T(8,128)(2,1)}, u32[]{:S(2)}) copy-start(bf16[8,1024]{1,0:T(8,128)(2,1)} %param.12) | copy-start | bytes 49156
  18.2 5.8 %copy-start.5 = (u32[32]{0:T(128)S(1)}, u32[32]{0:T(128)}, u32[]{:S(2)}) copy-start(u32[32]{0:T(128)} %constant.151) | copy-start | bytes 388
  24.6 8.8 %all-to-all-start.2 = ((s32[8,1,1,4]{3,2,1,0:T(1,128)}), s32[8,1,1,4]{3,2,1,0:T(1,128)S(1)}, u32[]{:S(2)}, u32[]{:S(2)}) async-start(s32[8,1,1,4]{3,2,1,0:T(1,128)} %copy.73), calls=%async_computation.2 | async-start | bytes 8192 | tf_op jit(solution)/shard_map/all_to_all | solution.py:134
  33.1 50.5 %copy-start.4 = (bf16[2,1024]{1,0:T(2,128)(2,1)S(1)}, bf16[2,1024]{1,0:T(2,128)(2,1)}, u32[]{:S(2)}) copy-start(bf16[2,1024]{1,0:T(2,128)(2,1)} %param.16) | copy-start | bytes 12292
  33.4 54.5 %all-to-all-start.1 = ((bf16[8,1,1,4,2,128,128]{6,5,3,4,2,1,0:T(8,128)(2,1)}), bf16[8,1,1,4,2,128,128]{6,5,3,4,2,1,0:T(8,128)(2,1)}, u32[]{:S(2)}, u32[]{:S(2)}) async-start(bf16[8,1,1,4,2,128,128]{6,5,3,4,2,1,0:T(8,128)(2,1)} %copy.69), calls=%async_computation.1 | async-start | bytes 4194304 | tf_op jit(solution)/shard_map/all_to_all | solution.py:136
  87.9 175.0 %all-to-all-start.3 = ((bf16[8,1,1,4,2,128,128]{6,5,3,4,2,1,0:T(8,128)(2,1)}), bf16[8,1,1,4,2,128,128]{6,5,3,4,2,1,0:T(8,128)(2,1)S(1)}, u32[]{:S(2)}, u32[]{:S(2)}) async-start(bf16[8,1,1,4,2,128,128]{6,5,3,4,2,1,0:T(8,128)(2,1)} %copy.76), calls=%async_computation.3 | async-start | bytes 4194304 | tf_op jit(solution)/shard_map/all_to_all | solution.py:136
  91.5 121.3 %all-reduce.15.cloned.1.call-start = ((), (), s32[]{:S(2)}) async-start(), calls=%async_computation.5 | async-start | bytes 458752 | tf_op jit(solution)/shard_map/psum | solution.py:152
  164.0 199.4 %all-reduce.13.cloned.1.call-start = ((), (), s32[]{:S(2)}) async-start(), calls=%async_computation.4 | async-start | bytes 458752 | tf_op jit(solution)/shard_map/psum | solution.py:152
  297.0 90.4 %copy-start.1 = (s32[1,32]{1,0:T(1,128)S(1)}, s32[1,32]{1,0:T(1,128)}, u32[]{:S(2)}) copy-start(s32[1,32]{1,0:T(1,128)} %param.21) | copy-start | bytes 388
Sparse Core Ops, SparseCore 0:
  164.1 48.5 all-reduce.14
  313.7 49.6 all-reduce.12
where the time goes:
time: 395 us; the launch traced here: 394 us
  blocking collectives  197 us (50%)
  waiting for transfers between devices  98.9 us (25%)
  matrix products  39.9 us (10%)
  local copies, waits for them, and re-layouts  19.7 us (5%)
  starting transfers between devices  17.4 us (4%)
  between operations  13.7 us (3%)
  other arithmetic  7.74 us (2%)
    psum x2, waiting for transfers between devices, shards(): totals = lax.psum((payload[0], payload[1]), 'req')  98.5 us
    psum x4, blocking collectives, sum_over_heads(): return lax.psum(partial_sum, 'tp')  73.2 us
    unnamed x2, blocking collectives  64.5 us
    all_gather x2, blocking collectives, shards(): lax.all_gather(context, 'req', axis=0, tiled=True)  35.7 us
    psum x2, blocking collectives, summed_inverse(): return inverse_of(lax.psum(local_squares(current), 'req'))  23.6 us
    dot_general x2, matrix products, shards(): jnp.dot(scaled, gate_weight[layer_no], preferred_element_type=jnp.float32)  9.57 us
    dot_general x2, matrix products, shards(): jnp.dot(scaled, up_weight[layer_no], preferred_element_type=jnp.float32)  9.57 us
    all_to_all x2, starting transfers between devices, shards(): lax.all_to_all(wanted, 'req', split_axis=0, concat_axis=0, tiled=True)  9.37 us
  transfers between devices with their start and end apart: 6, of which 3 were waited for; matrix products, arithmetic and copies ran while one was open for 11% of the time, Pallas kernels for 0%

commit v1 on v0

--- a/solution.py
+++ b/solution.py
@@ -1,8 +1,12 @@
+import functools
 import math
 
 import jax
 import jax.numpy as jnp
+import numpy as np
 from jax import lax
+from jax.experimental import pallas as pl
+from jax.experimental.pallas import tpu as pltpu
 from jax.sharding import PartitionSpec as P
 
 D = 8192
@@ -11,6 +15,11 @@
 
 MASK_FILL = -1e30
 EPSILON = 1e-05
+MESH = pl.DeviceIdType.MESH
+LANES = 128
+TOKENS = 512
+WIDE = 512
+MIB = 1 << 20
 
 
 def rotary(queries, position):
@@ -158,9 +167,427 @@
     return current
 
 
+def decoder_kernel(
+    n,
+    nt,
+    hidden_ref,
+    attn_gain_ref,
+    ffn_gain_ref,
+    used_ref,
+    turn_ref,
+    q_hbm,
+    o_hbm,
+    gate_hbm,
+    up_hbm,
+    down_hbm,
+    kv_hbm,
+    out_ref,
+    state,
+    q_w,
+    o_w,
+    gate_w,
+    up_w,
+    down_w,
+    kv_w,
+    used_all,
+    q_out,
+    q_in,
+    q_all,
+    scores,
+    part_out,
+    part_in,
+    ctx_all,
+    ffn_out,
+    ffn_in,
+    act_all,
+    head_sums,
+    load_sem,
+    send_sem,
+    recv_sem,
+    tp_send_sem,
+    tp_recv_sem,
+):
+    me = lax.axis_index("req")
+    my_tp = lax.axis_index("tp")
+    hd = LANES
+    slots = kv_w.shape[1]
+
+    def load(layer, which):
+        source, target = (
+            (q_hbm, q_w),
+            (kv_hbm, kv_w),
+            (o_hbm, o_w),
+            (gate_hbm, gate_w),
+            (up_hbm, up_w),
+            (down_hbm, down_w),
+        )[which]
+        if which == 1:
+            source = source.at[layer, :, 0]
+        else:
+            source = source.at[layer]
+        return pltpu.make_async_copy(source, target.at[layer], load_sem.at[layer, which])
+
+    def peer(step):
+        return lax.rem(me + step, n)
+
+    def send(source, target, step, phase):
+        return pltpu.make_async_remote_copy(
+            src_ref=source,
+            dst_ref=target,
+            send_sem=send_sem.at[step],
+            recv_sem=recv_sem.at[phase, me],
+            device_id=(peer(step), my_tp),
+            device_id_type=MESH,
+        )
+
+    def wait_from(slot, who, phase):
+        pltpu.make_async_remote_copy(
+            src_ref=slot,
+            dst_ref=slot,
+            send_sem=send_sem.at[0],
+            recv_sem=recv_sem.at[phase, who],
+            device_id=(who, my_tp),
+            device_id_type=MESH,
+        ).wait_recv()
+
+    def exchange(source_of, target, phase):
+        copies = [send(source_of(peer(step)), target.at[me], step, phase) for step in range(1, n)]
+        for copy in copies:
+            copy.start()
+        return copies
+
+    def finish(copies, target, phase):
+        for step in range(1, n):
+            who = peer(step)
+            wait_from(target.at[who], who, phase)
+        for copy in copies:
+            copy.wait_send()
+
+    def over_heads(buffer, phase):
+        copies = []
+        for step in range(1, nt):
+            copies.append(
+                pltpu.make_async_remote_copy(
+                    src_ref=buffer.at[my_tp],
+                    dst_ref=buffer.at[my_tp],
+                    send_sem=tp_send_sem.at[step],
+                    recv_sem=tp_recv_sem.at[phase, my_tp],
+                    device_id=(me, lax.rem(my_tp + step, nt)),
+                    device_id_type=MESH,
+                )
+            )
+        for copy in copies:
+            copy.start()
+        for step in range(1, nt):
+            who = lax.rem(my_tp + step, nt)
+            pltpu.make_async_remote_copy(
+                src_ref=buffer.at[who],
+                dst_ref=buffer.at[who],
+                send_sem=tp_send_sem.at[0],
+                recv_sem=tp_recv_sem.at[phase, who],
+                device_id=(me, who),
+                device_id_type=MESH,
+            ).wait_recv()
+        for copy in copies:
+            copy.wait_send()
+        total = buffer[0]
+        for index in range(1, nt):
+            total = total + buffer[index]
+        state[...] = (state[...] + total).astype(jnp.bfloat16).astype(jnp.float32)
+
+    def normed(gain_ref, layer):
+        current = state[...]
+        gains = gain_ref[...].astype(jnp.float32)
+        gain = jnp.where(layer == 0, gains[0:1], gains[1:2])
+        squares = jnp.sum(current * current, axis=1, keepdims=True)
+        return (current * gain).astype(jnp.bfloat16), jnp.broadcast_to(squares, (current.shape[0], LANES))
+
+    def ffn_start(who):
+        return pl.multiple_of((7 * who // 2) * LANES, LANES)
+
+    for which in range(3):
+        load(0, which).start()
+
+    barrier = pltpu.get_barrier_semaphore()
+    for step in range(1, n):
+        pl.semaphore_signal(barrier, inc=1, device_id=(peer(step), my_tp), device_id_type=MESH)
+    for step in range(1, nt):
+        pl.semaphore_signal(
+            barrier, inc=1, device_id=(me, lax.rem(my_tp + step, nt)), device_id_type=MESH
+        )
+    state[...] = hidden_ref[...].astype(jnp.float32)
+    used_all[me] = used_ref[me]
+    pl.semaphore_wait(barrier, n - 1 + nt - 1)
+
+    used_phase = 6 * LAYERS
+    used_copies = exchange(lambda who: used_ref.at[who], used_all, used_phase)
+    finish(used_copies, used_all, used_phase)
+
+    def layer_body(layer, carry):
+        phase = 6 * layer
+        scaled, squares = normed(attn_gain_ref, layer)
+        load(layer, 0).wait()
+        for pair in range(n // 2):
+            product = jnp.dot(
+                scaled,
+                q_w[layer, :, pair * 2 * hd : (pair + 1) * 2 * hd],
+                preferred_element_type=jnp.float32,
+            )
+            for half in range(2):
+                q_out[2 * pair + half, 0:8] = product[:, half * hd : (half + 1) * hd]
+                q_out[2 * pair + half, 8:16] = squares
+        copies = exchange(lambda who: q_out.at[who], q_in.at[layer], phase)
+        q_in[layer, me] = q_out[me]
+
+        @pl.when(layer == 0)
+        def _():
+            for which in range(3, 6):
+                load(0, which).start()
+
+        finish(copies, q_in.at[layer], phase)
+        total = q_in[layer, 0]
+        for who in range(1, n):
+            total = total + q_in[layer, who]
+        query = total[0:8] * lax.rsqrt(total[8:16] / D + EPSILON)
+        swapped = jnp.concatenate([query[:, hd // 2 :], query[:, : hd // 2]], axis=1)
+        query = (query * turn_ref[0:8] + swapped * turn_ref[8:16]) * hd ** (-0.5)
+        q_all[layer, me] = query.astype(jnp.bfloat16).astype(jnp.float32)
+        copies = exchange(lambda who: q_all.at[layer, me], q_all.at[layer], phase + 1)
+        rows8 = lax.broadcasted_iota(jnp.int32, (8, LANES), 0)
+        used = jnp.zeros((8, LANES), jnp.float32)
+        for who in range(n):
+            used = jnp.where(rows8 == who, used_all[who, layer], used)
+        load(layer, 1).wait()
+        finish(copies, q_all.at[layer], phase + 1)
+
+        queries = q_all[layer].reshape(n * 8, hd).astype(jnp.bfloat16)
+        step_slots = TOKENS // LANES
+        peak = jnp.full((n * 8, LANES), MASK_FILL, jnp.float32)
+        for chunk in range(slots // step_slots):
+            keys = kv_w[layer, chunk * step_slots : (chunk + 1) * step_slots, 0].reshape(TOKENS, hd)
+            block = lax.dot_general(
+                queries, keys, (((1,), (1,)), ((), ())), preferred_element_type=jnp.float32
+            )
+            for k in range(step_slots):
+                slot = chunk * step_slots + k
+                mask = jnp.broadcast_to(used[:, slot : slot + 1], (8, LANES)) > 0.5
+                mask = jnp.broadcast_to(mask[None], (n, 8, LANES))
+                piece = block[:, k * LANES : (k + 1) * LANES].reshape(n, 8, LANES)
+                piece = jnp.where(mask, piece, MASK_FILL).reshape(n * 8, LANES)
+                scores[:, slot * LANES : (slot + 1) * LANES] = piece
+                peak = jnp.maximum(peak, piece)
+        top = jnp.max(peak, axis=1, keepdims=True)
+        sums = jnp.zeros((n * 8, LANES), jnp.float32)
+        acc = jnp.zeros((n * 8, hd), jnp.float32)
+        for chunk in range(slots // step_slots):
+            terms = jnp.exp(scores[:, chunk * TOKENS : (chunk + 1) * TOKENS] - top)
+            for k in range(step_slots):
+                sums = sums + terms[:, k * LANES : (k + 1) * LANES]
+            values = kv_w[layer, chunk * step_slots : (chunk + 1) * step_slots, 1].reshape(TOKENS, hd)
+            acc = acc + jnp.dot(terms.astype(jnp.bfloat16), values, preferred_element_type=jnp.float32)
+        total = jnp.sum(sums, axis=1, keepdims=True)
+        lane = lax.broadcasted_iota(jnp.int32, (n * 8, LANES), 1)
+        stats = jnp.where(lane < LANES // 2, top, total)
+        for head in range(n):
+            part_out[head, 0:8] = acc[head * 8 : (head + 1) * 8]
+            part_out[head, 8:16] = stats[head * 8 : (head + 1) * 8]
+        copies = exchange(lambda who: part_out.at[who], part_in.at[layer], phase + 2)
+        part_in[layer, me] = part_out[me]
+        finish(copies, part_in.at[layer], phase + 2)
+
+        tops = [part_in[layer, who, 8:16][:, 0:1] for who in range(n)]
+        overall = functools.reduce(jnp.maximum, tops)
+        numerator = jnp.zeros((8, hd), jnp.float32)
+        denominator = jnp.zeros((8, 1), jnp.float32)
+        for who in range(n):
+            rescale = jnp.exp(tops[who] - overall)
+            numerator = numerator + rescale * part_in[layer, who, 0:8]
+            denominator = denominator + rescale * part_in[layer, who, 8:16][:, LANES // 2 : LANES // 2 + 1]
+        ctx_all[layer, me] = (numerator / denominator).astype(jnp.bfloat16).astype(jnp.float32)
+        copies = exchange(lambda who: ctx_all.at[layer, me], ctx_all.at[layer], phase + 3)
+        load(layer, 2).wait()
+        finish(copies, ctx_all.at[layer], phase + 3)
+
+        context = jnp.concatenate([ctx_all[layer, head] for head in range(n)], axis=1).astype(jnp.bfloat16)
+        for part in range(n // 2):
+            columns = slice(part * 256, (part + 1) * 256)
+            head_sums[layer, 0, my_tp, :, columns] = jnp.dot(
+                context, o_w[layer, :, columns], preferred_element_type=jnp.float32
+            )
+        over_heads(head_sums.at[layer, 0], 2 * layer)
+
+        scaled, squares = normed(ffn_gain_ref, layer)
+        load(layer, 3).wait()
+        load(layer, 4).wait()
+
+        def gate_up(who):
+            columns = pl.ds(ffn_start(who), WIDE)
+            ffn_out[who, :, 0:WIDE] = jnp.dot(
+                scaled, gate_w[layer, :, columns], preferred_element_type=jnp.float32
+            )
+            ffn_out[who, :, WIDE : 2 * WIDE] = jnp.dot(
+                scaled, up_w[layer, :, columns], preferred_element_type=jnp.float32
+            )
+            ffn_out[who, :, 2 * WIDE :] = squares
+
+        def ffn_step(step, carry):
+            who = peer(step)
+            gate_up(who)
+            send(ffn_out.at[who], ffn_in.at[layer, me], step, phase + 4).start()
+            return carry
+
+        lax.fori_loop(1, n, ffn_step, 0)
+
+        @pl.when(layer + 1 < LAYERS)
+        def _():
+            for which in range(6):
+                load(layer + 1, which).start()
+
+        gate_up(me)
+        ffn_in[layer, me] = ffn_out[me]
+        copies = [send(ffn_out.at[peer(step)], ffn_in.at[layer, me], step, phase + 4) for step in range(1, n)]
+        finish(copies, ffn_in.at[layer], phase + 4)
+        total = ffn_in[layer, 0]
+        for who in range(1, n):
+            total = total + ffn_in[layer, who]
+        inv = lax.rsqrt(total[:, 2 * WIDE :] / D + EPSILON)[:, 0:1]
+        gate = total[:, 0:WIDE] * inv
+        up = total[:, WIDE : 2 * WIDE] * inv
+        act = gate / (1.0 + jnp.exp(-gate)) * up
+        lane = lax.broadcasted_iota(jnp.int32, (8, WIDE), 1)
+        act = jnp.where(lane < lax.rem(me, 2) * LANES, 0.0, act)
+        packed = jnp.concatenate([act[:, 0 : WIDE // 2], act[:, WIDE // 2 :]], axis=0)
+        act_all[layer, me] = packed.astype(jnp.bfloat16)
+        copies = exchange(lambda who: act_all.at[layer, me], act_all.at[layer], phase + 5)
+        load(layer, 5).wait()
+
+        def down(who, total):
+            packed = act_all[layer, who].astype(jnp.float32)
+            act = jnp.concatenate([packed[0:8], packed[8:16]], axis=1).astype(jnp.bfloat16)
+            return total + jnp.dot(
+                act, down_w[layer, pl.ds(ffn_start(who), WIDE), :], preferred_element_type=jnp.float32
+            )
+
+        def down_step(step, total):
+            who = lax.rem(me + n - step, n)
+            wait_from(act_all.at[layer, who], who, phase + 5)
+            return down(who, total)
+
+        total = down(me, jnp.zeros(state.shape, jnp.float32))
+        head_sums[layer, 1, my_tp] = lax.fori_loop(1, n, down_step, total)
+        for copy in copies:
+            copy.wait_send()
+        over_heads(head_sums.at[layer, 1], 2 * layer + 1)
+        return carry
+
+    lax.fori_loop(0, LAYERS, layer_body, 0)
+    out_ref[...] = state[...].astype(out_ref.dtype)
+
+
+def rotary_table(head_size, position):
+    freq = np.arange(head_size // 2, dtype=np.float64)
+    angles = position * np.exp(freq * (-2.0 * math.log(500000.0) / head_size))
+    cosine = np.concatenate([np.cos(angles), np.cos(angles)])
+    sine = np.concatenate([-np.sin(angles), np.sin(angles)])
+    table = np.concatenate([np.tile(cosine[None], (8, 1)), np.tile(sine[None], (8, 1))])
+    return jnp.asarray(table, jnp.float32)
+
+
+def used_slots(block_home, chosen, chosen_count, n, pool_dev):
+    ctx = block_home.shape[1]
+    entries = jnp.arange(chosen.shape[3])
+    picked = (chosen[:, 0, 0, None, :] == jnp.arange(ctx)[None, :, None]) & (
+        entries < chosen_count[:, 0, 0, None, None]
+    )
+    picked = jnp.any(picked, axis=2)
+    local = jnp.arange(LANES)
+    slot_ids = jnp.where(local < pool_dev, jnp.arange(n)[:, None] * pool_dev + local, -1)
+    used = jnp.any(
+        picked[None, :, :, None] & (block_home[0][None, None, :, None] == slot_ids[:, None, None, :]), axis=2
+    )
+    used = used.astype(jnp.float32)
+    return jnp.broadcast_to(used[:, :, None, :], (n, used.shape[1], 8, LANES))
+
+
+def fused_shards(
+    n,
+    nt,
+    hidden,
+    attn_gain,
+    q_weight,
+    o_weight,
+    ffn_gain,
+    gate_weight,
+    up_weight,
+    down_weight,
+    kv_pool,
+    block_home,
+    chosen,
+    chosen_count,
+):
+    pool_dev = kv_pool.shape[1]
+    head_size = kv_pool.shape[5]
+    requests, features = hidden.shape
+    position = float(block_home.shape[1] * kv_pool.shape[4] - 1)
+    used = used_slots(block_home, chosen, chosen_count, n, pool_dev)
+    vmem = pl.BlockSpec(memory_space=pltpu.VMEM)
+    anywhere = pl.BlockSpec(memory_space=pl.ANY)
+    f32, bf16 = jnp.float32, jnp.bfloat16
+    return pl.pallas_call(
+        functools.partial(decoder_kernel, n, nt),
+        out_shape=jax.ShapeDtypeStruct(hidden.shape, hidden.dtype),
+        in_specs=[vmem] * 5 + [anywhere] * 6,
+        out_specs=vmem,
+        scratch_shapes=[
+            pltpu.VMEM((requests, features), f32),
+            pltpu.VMEM(q_weight.shape, bf16),
+            pltpu.VMEM(o_weight.shape, bf16),
+            pltpu.VMEM(gate_weight.shape, bf16),
+            pltpu.VMEM(up_weight.shape, bf16),
+            pltpu.VMEM(down_weight.shape, bf16),
+            pltpu.VMEM(kv_pool.shape[:2] + kv_pool.shape[3:], bf16),
+            pltpu.VMEM((n, LAYERS, 8, LANES), f32),
+            pltpu.VMEM((n, 16, LANES), f32),
+            pltpu.VMEM((LAYERS, n, 16, LANES), f32),
+            pltpu.VMEM((LAYERS, n, 8, LANES), f32),
+            pltpu.VMEM((8 * n, pool_dev * LANES), f32),
+            pltpu.VMEM((n, 16, LANES), f32),
+            pltpu.VMEM((LAYERS, n, 16, LANES), f32),
+            pltpu.VMEM((LAYERS, n, 8, LANES), f32),
+            pltpu.VMEM((n, 8, 2 * WIDE + LANES), f32),
+            pltpu.VMEM((LAYERS, n, 8, 2 * WIDE + LANES), f32),
+            pltpu.VMEM((LAYERS, n, 16, WIDE // 2), bf16),
+            pltpu.VMEM((LAYERS, 2, nt, requests, features), f32),
+            pltpu.SemaphoreType.DMA((LAYERS, 6)),
+            pltpu.SemaphoreType.DMA((n,)),
+            pltpu.SemaphoreType.DMA((6 * LAYERS + 1, n)),
+            pltpu.SemaphoreType.DMA((nt,)),
+            pltpu.SemaphoreType.DMA((2 * LAYERS, nt)),
+        ],
+        compiler_params=pltpu.CompilerParams(
+            collective_id=0, has_side_effects=True, vmem_limit_bytes=62 * MIB
+        ),
+        name="decoder_layers",
+    )(
+        hidden,
+        attn_gain,
+        ffn_gain,
+        used,
+        rotary_table(head_size, position),
+        q_weight,
+        o_weight,
+        gate_weight,
+        up_weight,
+        down_weight,
+        kv_pool,
+    )
+
+
 def solution(mesh):
+    n, nt = mesh.shape["req"], mesh.shape["tp"]
+    body = functools.partial(fused_shards, n, nt) if n == 8 else shards
     return jax.shard_map(
-        shards,
+        body,
         mesh=mesh,
         in_specs=(
             P(None, "req"),

time: 395 us -> 85.4 us (0.22)
  blocking collectives: 197 us -> 0 us
  waiting for transfers between devices: 98.9 us -> 0 us
  Pallas kernels: 0 us -> 80.7 us
  matrix products: 39.9 us -> 0 us
  local copies, waits for them, and re-layouts: 19.7 us -> 1.95 us
  starting transfers between devices: 17.4 us -> 0 us
  between operations: 13.7 us -> 0.04 us
  other arithmetic: 7.74 us -> 2.44 us
    psum x2 -> x0, waiting for transfers between devices: 98.5 us -> none  [shards(): totals = lax.psum((payload[0], payload[1]), 'req')]
    psum x6 -> x0, blocking collectives: 96.7 us -> none  [the longest x4 73.2 us: sum_over_heads(): return lax.psum(partial_sum, 'tp')]
    pallas_call x0 -> x1, Pallas kernels: none -> 80.7 us  [fused_shards(): pl.pallas_call(functools.partial(decoder_kernel, n, nt), out_shape=jax.Sh...]
    unnamed x2 -> x0, blocking collectives: 64.5 us -> none
    dot_general x14 -> x0, matrix products: 39.9 us -> none  [the longest x2 9.57 us: shards(): jnp.dot(scaled, gate_weight[layer_no], preferred_element_type=jnp.float32)]
    all_gather x2 -> x0, blocking collectives: 35.7 us -> none  [shards(): lax.all_gather(context, 'req', axis=0, tiled=True)]
    all_to_all x4 -> x0, starting transfers between devices: 17.3 us -> none  [the longest x2 9.37 us: shards(): lax.all_to_all(wanted, 'req', split_axis=0, concat_axis=0, tiled=True)]
    gather x6 -> x0, local copies, waits for them, and re-layouts: 9.51 us -> none  [the longest x4 8.04 us: shards(): served = kv_pool[layer_no][jnp.maximum(received_ids, 0), head_index]]
  transfers between devices with their start and end apart: 6 -> 0, of which waited for: 3 -> 0; matrix products, arithmetic and copies ran while one was open for 11% -> 0% of each run, Pallas kernels for 0% -> 0%
where the time goes in v1:
time: 85.4 us; the launch traced here: 85.1 us
  Pallas kernels  80.7 us (94%)
  other arithmetic  2.44 us (3%)
  local copies, waits for them, and re-layouts  1.95 us (2%)
    pallas_call x1, Pallas kernels, fused_shards(): pl.pallas_call(functools.partial(decoder_kernel, n, nt), out_shape=jax.Sh...  80.7 us

profile of v1, /device:TPU:0, one launch (start us, length us, event | category | flops | bytes accessed | tf_op | source)
XLA Modules:
  0.0 85.1 jit_solution(15165685251035121271)
XLA Ops:
  0.0 0.7 iota_compare_fusion.1
  0.7 0.8 fusion.1
  1.5 0.1 add_select_fusion
  1.6 0.7 broadcast_compare_fusion
  2.3 0.1 and_reduce_fusion
  2.5 0.6 broadcast_in_dim.12.used_ref
  3.1 80.7 %decoder_layers.1 = bf16[8,1024]{1,0:T(8,128)(2,1)} custom-call(bf16[8,1024]{1,0:T(8,128)(2,1)} %hidden_ref.1, bf16[2,1024]{1,0:T(2,128)(2,1)} %attn_gain_ref.1, bf16[2,1024]{1,0:T(2,128)(2,1)} %ffn_gain_ref.1, f32[8,2,8,128]{3,2,1,0:T(8,128)} %broadcast_in_dim.12.used_ref, f32[16,128]{1,0:T(8,128)} %constant.3.clone.turn_ref, bf16[2,1024,1024]{2,1,0:T(8,128)(2,1)} %q_hbm.1, ...), custom_call_target="tpu_custom_call" | custom-call | tf_op jit(solution)/shard_map/decoder_layers/pallas_call | solution.py:536
  83.8 1.3 %copy.15 = bf16[8,1024]{1,0:T(8,128)(2,1)} copy(bf16[8,1024]{1,0:T(8,128)(2,1)} %decoder_layers.1) | data formatting | bytes 32768
  (3 shorter events, 0.0 us)

commit v2 on v1

--- a/solution.py
+++ b/solution.py
@@ -19,6 +19,7 @@
 LANES = 128
 TOKENS = 512
 WIDE = 512
+PARTS = 2
 MIB = 1 << 20
 
 
@@ -173,8 +174,10 @@
     hidden_ref,
     attn_gain_ref,
     ffn_gain_ref,
-    used_ref,
     turn_ref,
+    home_ref,
+    chosen_ref,
+    count_ref,
     q_hbm,
     o_hbm,
     gate_hbm,
@@ -189,6 +192,7 @@
     up_w,
     down_w,
     kv_w,
+    used_out,
     used_all,
     q_out,
     q_in,
@@ -204,6 +208,7 @@
     load_sem,
     send_sem,
     recv_sem,
+    used_sem,
     tp_send_sem,
     tp_recv_sem,
 ):
@@ -263,37 +268,40 @@
         for copy in copies:
             copy.wait_send()
 
-    def over_heads(buffer, phase):
+    def head_copy(slot, step, phase, part, who):
+        return pltpu.make_async_remote_copy(
+            src_ref=slot,
+            dst_ref=slot,
+            send_sem=tp_send_sem.at[part, step],
+            recv_sem=tp_recv_sem.at[phase, part, who],
+            device_id=(me, lax.rem(my_tp + step, nt)),
+            device_id_type=MESH,
+        )
+
+    def over_heads(product_of, buffer, phase):
         copies = []
-        for step in range(1, nt):
-            copies.append(
-                pltpu.make_async_remote_copy(
-                    src_ref=buffer.at[my_tp],
-                    dst_ref=buffer.at[my_tp],
-                    send_sem=tp_send_sem.at[step],
-                    recv_sem=tp_recv_sem.at[phase, my_tp],
-                    device_id=(me, lax.rem(my_tp + step, nt)),
-                    device_id_type=MESH,
-                )
-            )
-        for copy in copies:
-            copy.start()
-        for step in range(1, nt):
-            who = lax.rem(my_tp + step, nt)
-            pltpu.make_async_remote_copy(
-                src_ref=buffer.at[who],
-                dst_ref=buffer.at[who],
-                send_sem=tp_send_sem.at[0],
-                recv_sem=tp_recv_sem.at[phase, who],
-                device_id=(me, who),
-                device_id_type=MESH,
-            ).wait_recv()
+        for part in range(PARTS):
+            product = product_of(part)
+            width = product.shape[1] // 2
+            packed = jnp.concatenate([product[:, :width], product[:, width:]], axis=0)
+            buffer[my_tp, part] = packed.astype(jnp.bfloat16)
+            for step in range(nt - 1, 0, -1):
+                copy = head_copy(buffer.at[my_tp, part], step, phase, part, my_tp)
+                copy.start()
+                copies.append(copy)
+        for part in range(PARTS):
+            for step in range(1, nt):
+                who = lax.rem(my_tp + step, nt)
+                head_copy(buffer.at[who, part], step, phase, part, who).wait_recv()
+            total = buffer[0, part].astype(jnp.float32)
+            for index in range(1, nt):
+                total = total + buffer[index, part].astype(jnp.float32)
+            total = jnp.concatenate([total[0:8], total[8:16]], axis=1)
+            width = total.shape[1]
+            columns = slice(part * width, (part + 1) * width)
+            state[:, columns] = (state[:, columns] + total).astype(jnp.bfloat16).astype(jnp.float32)
         for copy in copies:
             copy.wait_send()
-        total = buffer[0]
-        for index in range(1, nt):
-            total = total + buffer[index]
-        state[...] = (state[...] + total).astype(jnp.bfloat16).astype(jnp.float32)
 
     def normed(gain_ref, layer):
         current = state[...]
@@ -316,15 +324,8 @@
             barrier, inc=1, device_id=(me, lax.rem(my_tp + step, nt)), device_id_type=MESH
         )
     state[...] = hidden_ref[...].astype(jnp.float32)
-    used_all[me] = used_ref[me]
-    pl.semaphore_wait(barrier, n - 1 + nt - 1)
-
-    used_phase = 6 * LAYERS
-    used_copies = exchange(lambda who: used_ref.at[who], used_all, used_phase)
-    finish(used_copies, used_all, used_phase)
-
-    def layer_body(layer, carry):
-        phase = 6 * layer
+
+    def query_product(layer):
         scaled, squares = normed(attn_gain_ref, layer)
         load(layer, 0).wait()
         for pair in range(n // 2):
@@ -336,13 +337,42 @@
             for half in range(2):
                 q_out[2 * pair + half, 0:8] = product[:, half * hd : (half + 1) * hd]
                 q_out[2 * pair + half, 8:16] = squares
+
+    rows8 = lax.broadcasted_iota(jnp.int32, (n, LANES), 0)
+    lanes8 = lax.broadcasted_iota(jnp.int32, (n, LANES), 1)
+    slot_ids = jnp.where(lanes8 < slots, rows8 * slots + lanes8, -1)
+    for layer in range(LAYERS):
+        used = jnp.zeros((n, LANES), jnp.float32)
+        for entry in range(chosen_ref.shape[3]):
+            slot = home_ref[0, chosen_ref[layer, 0, 0, entry]]
+            slot = jnp.where(entry < count_ref[layer, 0, 0], slot, -2)
+            used = jnp.where(slot_ids == slot, 1.0, used)
+        used_out[layer] = used
+    query_product(0)
+    for which in range(3, 6):
+        load(0, which).start()
+    pl.semaphore_wait(barrier, n - 1 + nt - 1)
+
+    def used_copy(step):
+        return pltpu.make_async_remote_copy(
+            src_ref=used_out,
+            dst_ref=used_all.at[me],
+            send_sem=used_sem.at[step],
+            recv_sem=recv_sem.at[6 * LAYERS, me],
+            device_id=(peer(step), my_tp),
+            device_id_type=MESH,
+        )
+
+    def layer_body(layer, carry):
+        phase = 6 * layer
         copies = exchange(lambda who: q_out.at[who], q_in.at[layer], phase)
         q_in[layer, me] = q_out[me]
 
         @pl.when(layer == 0)
         def _():
-            for which in range(3, 6):
-                load(0, which).start()
+            for step in range(1, n):
+                used_copy(step).start()
+            used_all[me] = used_out[...]
 
         finish(copies, q_in.at[layer], phase)
         total = q_in[layer, 0]
@@ -353,10 +383,17 @@
         query = (query * turn_ref[0:8] + swapped * turn_ref[8:16]) * hd ** (-0.5)
         q_all[layer, me] = query.astype(jnp.bfloat16).astype(jnp.float32)
         copies = exchange(lambda who: q_all.at[layer, me], q_all.at[layer], phase + 1)
-        rows8 = lax.broadcasted_iota(jnp.int32, (8, LANES), 0)
+
+        @pl.when(layer == 0)
+        def _():
+            for step in range(1, n):
+                wait_from(used_all.at[peer(step)], peer(step), 6 * LAYERS)
+                used_copy(step).wait_send()
+
         used = jnp.zeros((8, LANES), jnp.float32)
         for who in range(n):
-            used = jnp.where(rows8 == who, used_all[who, layer], used)
+            row = jnp.where(rows8 == me, used_all[who, layer], 0.0)
+            used = jnp.where(rows8 == who, jnp.sum(row, axis=0, keepdims=True), used)
         load(layer, 1).wait()
         finish(copies, q_all.at[layer], phase + 1)
 
@@ -409,12 +446,13 @@
         finish(copies, ctx_all.at[layer], phase + 3)
 
         context = jnp.concatenate([ctx_all[layer, head] for head in range(n)], axis=1).astype(jnp.bfloat16)
-        for part in range(n // 2):
-            columns = slice(part * 256, (part + 1) * 256)
-            head_sums[layer, 0, my_tp, :, columns] = jnp.dot(
-                context, o_w[layer, :, columns], preferred_element_type=jnp.float32
-            )
-        over_heads(head_sums.at[layer, 0], 2 * layer)
+        width = state.shape[1] // PARTS
+
+        def out_part(part):
+            weight = o_w[layer, :, part * width : (part + 1) * width]
+            return jnp.dot(context, weight, preferred_element_type=jnp.float32)
+
+        over_heads(out_part, head_sums.at[layer, 0], 2 * layer)
 
         scaled, squares = normed(ffn_gain_ref, layer)
         load(layer, 3).wait()
@@ -454,30 +492,29 @@
         gate = total[:, 0:WIDE] * inv
         up = total[:, WIDE : 2 * WIDE] * inv
         act = gate / (1.0 + jnp.exp(-gate)) * up
-        lane = lax.broadcasted_iota(jnp.int32, (8, WIDE), 1)
-        act = jnp.where(lane < lax.rem(me, 2) * LANES, 0.0, act)
         packed = jnp.concatenate([act[:, 0 : WIDE // 2], act[:, WIDE // 2 :]], axis=0)
         act_all[layer, me] = packed.astype(jnp.bfloat16)
         copies = exchange(lambda who: act_all.at[layer, me], act_all.at[layer], phase + 5)
         load(layer, 5).wait()
 
-        def down(who, total):
+        finish(copies, act_all.at[layer], phase + 5)
+        shares = []
+        for who in range(n):
             packed = act_all[layer, who].astype(jnp.float32)
-            act = jnp.concatenate([packed[0:8], packed[8:16]], axis=1).astype(jnp.bfloat16)
-            return total + jnp.dot(
-                act, down_w[layer, pl.ds(ffn_start(who), WIDE), :], preferred_element_type=jnp.float32
-            )
-
-        def down_step(step, total):
-            who = lax.rem(me + n - step, n)
-            wait_from(act_all.at[layer, who], who, phase + 5)
-            return down(who, total)
-
-        total = down(me, jnp.zeros(state.shape, jnp.float32))
-        head_sums[layer, 1, my_tp] = lax.fori_loop(1, n, down_step, total)
-        for copy in copies:
-            copy.wait_send()
-        over_heads(head_sums.at[layer, 1], 2 * layer + 1)
+            share = jnp.concatenate([packed[0:8], packed[8:16]], axis=1)
+            shares.append(share[:, (who % 2) * LANES :])
+        act = jnp.concatenate(shares, axis=1).astype(jnp.bfloat16)
+
+        def down_part(part):
+            weight = down_w[layer, :, part * width : (part + 1) * width]
+            return jnp.dot(act, weight, preferred_element_type=jnp.float32)
+
+        over_heads(down_part, head_sums.at[layer, 1], 2 * layer + 1)
+
+        @pl.when(layer + 1 < LAYERS)
+        def _():
+            query_product(layer + 1)
+
         return carry
 
     lax.fori_loop(0, LAYERS, layer_body, 0)
@@ -491,22 +528,6 @@
     sine = np.concatenate([-np.sin(angles), np.sin(angles)])
     table = np.concatenate([np.tile(cosine[None], (8, 1)), np.tile(sine[None], (8, 1))])
     return jnp.asarray(table, jnp.float32)
-
-
-def used_slots(block_home, chosen, chosen_count, n, pool_dev):
-    ctx = block_home.shape[1]
-    entries = jnp.arange(chosen.shape[3])
-    picked = (chosen[:, 0, 0, None, :] == jnp.arange(ctx)[None, :, None]) & (
-        entries < chosen_count[:, 0, 0, None, None]
-    )
-    picked = jnp.any(picked, axis=2)
-    local = jnp.arange(LANES)
-    slot_ids = jnp.where(local < pool_dev, jnp.arange(n)[:, None] * pool_dev + local, -1)
-    used = jnp.any(
-        picked[None, :, :, None] & (block_home[0][None, None, :, None] == slot_ids[:, None, None, :]), axis=2
-    )
-    used = used.astype(jnp.float32)
-    return jnp.broadcast_to(used[:, :, None, :], (n, used.shape[1], 8, LANES))
 
 
 def fused_shards(
@@ -529,14 +550,14 @@
     head_size = kv_pool.shape[5]
     requests, features = hidden.shape
     position = float(block_home.shape[1] * kv_pool.shape[4] - 1)
-    used = used_slots(block_home, chosen, chosen_count, n, pool_dev)
     vmem = pl.BlockSpec(memory_space=pltpu.VMEM)
+    scalars = pl.BlockSpec(memory_space=pltpu.SMEM)
     anywhere = pl.BlockSpec(memory_space=pl.ANY)
     f32, bf16 = jnp.float32, jnp.bfloat16
     return pl.pallas_call(
         functools.partial(decoder_kernel, n, nt),
         out_shape=jax.ShapeDtypeStruct(hidden.shape, hidden.dtype),
-        in_specs=[vmem] * 5 + [anywhere] * 6,
+        in_specs=[vmem] * 4 + [scalars] * 3 + [anywhere] * 6,
         out_specs=vmem,
         scratch_shapes=[
             pltpu.VMEM((requests, features), f32),
@@ -546,7 +567,8 @@
             pltpu.VMEM(up_weight.shape, bf16),
             pltpu.VMEM(down_weight.shape, bf16),
             pltpu.VMEM(kv_pool.shape[:2] + kv_pool.shape[3:], bf16),
-            pltpu.VMEM((n, LAYERS, 8, LANES), f32),
+            pltpu.VMEM((LAYERS, n, LANES), f32),
+            pltpu.VMEM((n, LAYERS, n, LANES), f32),
             pltpu.VMEM((n, 16, LANES), f32),
             pltpu.VMEM((LAYERS, n, 16, LANES), f32),
             pltpu.VMEM((LAYERS, n, 8, LANES), f32),
@@ -557,12 +579,13 @@
             pltpu.VMEM((n, 8, 2 * WIDE + LANES), f32),
             pltpu.VMEM((LAYERS, n, 8, 2 * WIDE + LANES), f32),
             pltpu.VMEM((LAYERS, n, 16, WIDE // 2), bf16),
-            pltpu.VMEM((LAYERS, 2, nt, requests, features), f32),
+            pltpu.VMEM((LAYERS, 2, nt, PARTS, 16, features // PARTS // 2), bf16),
             pltpu.SemaphoreType.DMA((LAYERS, 6)),
             pltpu.SemaphoreType.DMA((n,)),
             pltpu.SemaphoreType.DMA((6 * LAYERS + 1, n)),
-            pltpu.SemaphoreType.DMA((nt,)),
-            pltpu.SemaphoreType.DMA((2 * LAYERS, nt)),
+            pltpu.SemaphoreType.DMA((n,)),
+            pltpu.SemaphoreType.DMA((PARTS, nt)),
+            pltpu.SemaphoreType.DMA((2 * LAYERS, PARTS, nt)),
         ],
         compiler_params=pltpu.CompilerParams(
             collective_id=0, has_side_effects=True, vmem_limit_bytes=62 * MIB
@@ -572,8 +595,10 @@
         hidden,
         attn_gain,
         ffn_gain,
-        used,
         rotary_table(head_size, position),
+        block_home,
+        chosen,
+        chosen_count,
         q_weight,
         o_weight,
         gate_weight,

time: 85.4 us -> 75.6 us (0.89)
  Pallas kernels: 80.7 us -> 72.7 us
  other arithmetic: 2.44 us -> 0 us
    pallas_call x1, Pallas kernels: 80.7 us -> 72.7 us  [fused_shards(): pl.pallas_call(functools.partial(decoder_kernel, n, nt), out_shape=jax.Sh...]
    unnamed x1 -> x2, local copies, waits for them, and re-layouts: 1.32 us -> 2.62 us
    reduce_or x2 -> x0, other arithmetic: 0.88 us -> none  [the longest x1 0.77 us: used_slots(): picked = jnp.any(picked, axis=2)]
where the time goes in v2:
time: 75.6 us; the launch traced here: 75.3 us
  Pallas kernels  72.7 us (96%)
  local copies, waits for them, and re-layouts  2.62 us (3%)
    pallas_call x1, Pallas kernels, fused_shards(): pl.pallas_call(functools.partial(decoder_kernel, n, nt), out_shape=jax.Sh...  72.7 us
    unnamed x2, local copies, waits for them, and re-layouts  2.62 us

profile of v2, /device:TPU:0, one launch (start us, length us, event | category | flops | bytes accessed | tf_op | source)
XLA Modules:
  0.0 75.3 jit_solution(10524726543963650201)
XLA Ops:
  0.0 1.3 %copy.14.count_ref = s32[2,1,1]{2,1,0:T(1,128)} copy(s32[2,1,1]{0,2,1:T(1,128)} %param.24) | data formatting | bytes 16 | tf_op args[11]
  1.3 72.7 %decoder_layers.1 = bf16[8,1024]{1,0:T(8,128)(2,1)} custom-call(bf16[8,1024]{1,0:T(8,128)(2,1)} %hidden_ref.1, bf16[2,1024]{1,0:T(2,128)(2,1)} %attn_gain_ref.1, bf16[2,1024]{1,0:T(2,128)(2,1)} %ffn_gain_ref.1, f32[16,128]{1,0:T(8,128)} %constant.2.clone.turn_ref, s32[1,32]{1,0:T(1,128)} %home_ref.1, s32[2,1,1,24]{3,2,1,0:T(1,128)} %chosen_ref.1, ...), custom_call_target="tpu_custom_call" | custom-call | tf_op jit(solution)/shard_map/decoder_layers/pallas_call | solution.py:557
  74.0 1.3 %copy.16 = bf16[8,1024]{1,0:T(8,128)(2,1)} copy(bf16[8,1024]{1,0:T(8,128)(2,1)} %decoder_layers.1) | data formatting | bytes 32768

commit v3 on v2

--- a/solution.py
+++ b/solution.py
@@ -20,6 +20,7 @@
 TOKENS = 512
 WIDE = 512
 PARTS = 2
+PHASES = 5
 MIB = 1 << 20
 
 
@@ -194,13 +195,9 @@
     kv_w,
     used_out,
     used_all,
-    q_out,
     q_in,
-    q_all,
     scores,
-    part_out,
     part_in,
-    ctx_all,
     ffn_out,
     ffn_in,
     act_all,
@@ -209,12 +206,14 @@
     send_sem,
     recv_sem,
     used_sem,
+    q_send_sem,
     tp_send_sem,
     tp_recv_sem,
 ):
     me = lax.axis_index("req")
     my_tp = lax.axis_index("tp")
     hd = LANES
+    order = [*range(2, n), 1]
     slots = kv_w.shape[1]
 
     def load(layer, which):
@@ -256,7 +255,7 @@
         ).wait_recv()
 
     def exchange(source_of, target, phase):
-        copies = [send(source_of(peer(step)), target.at[me], step, phase) for step in range(1, n)]
+        copies = [send(source_of(peer(step)), target.at[me], step, phase) for step in order]
         for copy in copies:
             copy.start()
         return copies
@@ -325,18 +324,36 @@
         )
     state[...] = hidden_ref[...].astype(jnp.float32)
 
-    def query_product(layer):
+    def query_copies(layer, part):
+        return [
+            pltpu.make_async_remote_copy(
+                src_ref=q_in.at[layer, me, part],
+                dst_ref=q_in.at[layer, me, part],
+                send_sem=q_send_sem.at[part, step],
+                recv_sem=recv_sem.at[PHASES * layer + part, me],
+                device_id=(peer(step), my_tp),
+                device_id_type=MESH,
+            )
+            for step in order
+        ]
+
+    def query_product(layer, sending):
         scaled, squares = normed(attn_gain_ref, layer)
         load(layer, 0).wait()
-        for pair in range(n // 2):
+        high = squares.astype(jnp.bfloat16).astype(jnp.float32)
+        tail = jnp.concatenate([high, squares - high], axis=0)
+        width = q_w.shape[2] // PARTS
+        for part in range(PARTS):
             product = jnp.dot(
                 scaled,
-                q_w[layer, :, pair * 2 * hd : (pair + 1) * 2 * hd],
+                q_w[layer, :, part * width : (part + 1) * width],
                 preferred_element_type=jnp.float32,
             )
-            for half in range(2):
-                q_out[2 * pair + half, 0:8] = product[:, half * hd : (half + 1) * hd]
-                q_out[2 * pair + half, 8:16] = squares
+            packed = jnp.concatenate([product[:, : width // 2], product[:, width // 2 :]], axis=0)
+            q_in[layer, me, part] = jnp.concatenate([packed, tail], axis=1).astype(jnp.bfloat16)
+            if sending:
+                for copy in query_copies(layer, part):
+                    copy.start()
 
     rows8 = lax.broadcasted_iota(jnp.int32, (n, LANES), 0)
     lanes8 = lax.broadcasted_iota(jnp.int32, (n, LANES), 1)
@@ -345,10 +362,10 @@
         used = jnp.zeros((n, LANES), jnp.float32)
         for entry in range(chosen_ref.shape[3]):
             slot = home_ref[0, chosen_ref[layer, 0, 0, entry]]
-            slot = jnp.where(entry < count_ref[layer, 0, 0], slot, -2)
+            slot = jnp.where(entry < count_ref[0, 0, layer], slot, -2)
             used = jnp.where(slot_ids == slot, 1.0, used)
         used_out[layer] = used
-    query_product(0)
+    query_product(0, False)
     for which in range(3, 6):
         load(0, which).start()
     pl.semaphore_wait(barrier, n - 1 + nt - 1)
@@ -358,46 +375,55 @@
             src_ref=used_out,
             dst_ref=used_all.at[me],
             send_sem=used_sem.at[step],
-            recv_sem=recv_sem.at[6 * LAYERS, me],
+            recv_sem=recv_sem.at[PHASES * LAYERS, me],
             device_id=(peer(step), my_tp),
             device_id_type=MESH,
         )
 
+    for part in range(PARTS):
+        for copy in query_copies(0, part):
+            copy.start()
+    for step in order:
+        used_copy(step).start()
+    used_all[me] = used_out[...]
+
     def layer_body(layer, carry):
-        phase = 6 * layer
-        copies = exchange(lambda who: q_out.at[who], q_in.at[layer], phase)
-        q_in[layer, me] = q_out[me]
+        phase = PHASES * layer
+        load(layer, 1).wait()
 
         @pl.when(layer == 0)
         def _():
             for step in range(1, n):
-                used_copy(step).start()
-            used_all[me] = used_out[...]
-
-        finish(copies, q_in.at[layer], phase)
-        total = q_in[layer, 0]
-        for who in range(1, n):
-            total = total + q_in[layer, who]
-        query = total[0:8] * lax.rsqrt(total[8:16] / D + EPSILON)
-        swapped = jnp.concatenate([query[:, hd // 2 :], query[:, : hd // 2]], axis=1)
-        query = (query * turn_ref[0:8] + swapped * turn_ref[8:16]) * hd ** (-0.5)
-        q_all[layer, me] = query.astype(jnp.bfloat16).astype(jnp.float32)
-        copies = exchange(lambda who: q_all.at[layer, me], q_all.at[layer], phase + 1)
-
-        @pl.when(layer == 0)
-        def _():
-            for step in range(1, n):
-                wait_from(used_all.at[peer(step)], peer(step), 6 * LAYERS)
+                wait_from(used_all.at[peer(step)], peer(step), PHASES * LAYERS)
                 used_copy(step).wait_send()
 
         used = jnp.zeros((8, LANES), jnp.float32)
         for who in range(n):
             row = jnp.where(rows8 == me, used_all[who, layer], 0.0)
             used = jnp.where(rows8 == who, jnp.sum(row, axis=0, keepdims=True), used)
-        load(layer, 1).wait()
-        finish(copies, q_all.at[layer], phase + 1)
-
-        queries = q_all[layer].reshape(n * 8, hd).astype(jnp.bfloat16)
+        heads = []
+        for part in range(PARTS):
+            for step in range(1, n):
+                who = peer(step)
+                wait_from(q_in.at[layer, who, part], who, phase + part)
+            total = q_in[layer, 0, part].astype(jnp.float32)
+            for who in range(1, n):
+                total = total + q_in[layer, who, part].astype(jnp.float32)
+            width = total.shape[1] - LANES
+            squares = total[0:8, width:] + total[8:16, width:]
+            inv = lax.rsqrt(squares / D + EPSILON)
+            for half in range(2):
+                for head in range(width // hd):
+                    heads.append(total[half * 8 : half * 8 + 8, head * hd : (head + 1) * hd] * inv)
+        queries = []
+        for query in heads:
+            swapped = jnp.concatenate([query[:, hd // 2 :], query[:, : hd // 2]], axis=1)
+            queries.append((query * turn_ref[0:8] + swapped * turn_ref[8:16]) * hd ** (-0.5))
+        queries = jnp.concatenate(queries, axis=0).astype(jnp.bfloat16)
+        for part in range(PARTS):
+            for copy in query_copies(layer, part):
+                copy.wait_send()
+
         step_slots = TOKENS // LANES
         peak = jnp.full((n * 8, LANES), MASK_FILL, jnp.float32)
         for chunk in range(slots // step_slots):
@@ -423,29 +449,34 @@
             values = kv_w[layer, chunk * step_slots : (chunk + 1) * step_slots, 1].reshape(TOKENS, hd)
             acc = acc + jnp.dot(terms.astype(jnp.bfloat16), values, preferred_element_type=jnp.float32)
         total = jnp.sum(sums, axis=1, keepdims=True)
-        lane = lax.broadcasted_iota(jnp.int32, (n * 8, LANES), 1)
-        stats = jnp.where(lane < LANES // 2, top, total)
+        level = top + jnp.log(total)
+        stats = jnp.zeros((8, LANES), jnp.float32)
+        lane = lax.broadcasted_iota(jnp.int32, (8, LANES), 1)
         for head in range(n):
-            part_out[head, 0:8] = acc[head * 8 : (head + 1) * 8]
-            part_out[head, 8:16] = stats[head * 8 : (head + 1) * 8]
-        copies = exchange(lambda who: part_out.at[who], part_in.at[layer], phase + 2)
-        part_in[layer, me] = part_out[me]
+            stats = jnp.where(lane == head, level[head * 8 : (head + 1) * 8], stats)
+        high = stats.astype(jnp.bfloat16).astype(jnp.float32)
+        payload = jnp.concatenate([acc / total, high, stats - high], axis=0)
+        part_in[layer, me] = payload.astype(jnp.bfloat16)
+        copies = exchange(lambda who: part_in.at[layer, me], part_in.at[layer], phase + 2)
+        load(layer, 2).wait()
         finish(copies, part_in.at[layer], phase + 2)
 
-        tops = [part_in[layer, who, 8:16][:, 0:1] for who in range(n)]
-        overall = functools.reduce(jnp.maximum, tops)
-        numerator = jnp.zeros((8, hd), jnp.float32)
-        denominator = jnp.zeros((8, 1), jnp.float32)
+        rows = 8 * n
+        levels = []
         for who in range(n):
-            rescale = jnp.exp(tops[who] - overall)
-            numerator = numerator + rescale * part_in[layer, who, 0:8]
-            denominator = denominator + rescale * part_in[layer, who, 8:16][:, LANES // 2 : LANES // 2 + 1]
-        ctx_all[layer, me] = (numerator / denominator).astype(jnp.bfloat16).astype(jnp.float32)
-        copies = exchange(lambda who: ctx_all.at[layer, me], ctx_all.at[layer], phase + 3)
-        load(layer, 2).wait()
-        finish(copies, ctx_all.at[layer], phase + 3)
-
-        context = jnp.concatenate([ctx_all[layer, head] for head in range(n)], axis=1).astype(jnp.bfloat16)
+            pair = part_in[layer, who, rows : rows + 16].astype(jnp.float32)
+            levels.append(pair[0:8] + pair[8:16])
+        overall = functools.reduce(jnp.maximum, levels)
+        shares = [jnp.exp(level - overall) for level in levels]
+        denominator = functools.reduce(jnp.add, shares)
+        context = [jnp.zeros((8, hd), jnp.float32) for _ in range(n)]
+        for who in range(n):
+            share = shares[who] / denominator
+            parts = part_in[layer, who, 0:rows].astype(jnp.float32)
+            for head in range(n):
+                context[head] = context[head] + share[:, head : head + 1] * parts[head * 8 : (head + 1) * 8]
+        context = jnp.concatenate(context, axis=1).astype(jnp.bfloat16)
+
         width = state.shape[1] // PARTS
 
         def out_part(part):
@@ -471,7 +502,7 @@
         def ffn_step(step, carry):
             who = peer(step)
             gate_up(who)
-            send(ffn_out.at[who], ffn_in.at[layer, me], step, phase + 4).start()
+            send(ffn_out.at[who], ffn_in.at[layer, me], step, phase + 3).start()
             return carry
 
         lax.fori_loop(1, n, ffn_step, 0)
@@ -483,8 +514,8 @@
 
         gate_up(me)
         ffn_in[layer, me] = ffn_out[me]
-        copies = [send(ffn_out.at[peer(step)], ffn_in.at[layer, me], step, phase + 4) for step in range(1, n)]
-        finish(copies, ffn_in.at[layer], phase + 4)
+        copies = [send(ffn_out.at[peer(step)], ffn_in.at[layer, me], step, phase + 3) for step in range(1, n)]
+        finish(copies, ffn_in.at[layer], phase + 3)
         total = ffn_in[layer, 0]
         for who in range(1, n):
             total = total + ffn_in[layer, who]
@@ -494,10 +525,10 @@
         act = gate / (1.0 + jnp.exp(-gate)) * up
         packed = jnp.concatenate([act[:, 0 : WIDE // 2], act[:, WIDE // 2 :]], axis=0)
         act_all[layer, me] = packed.astype(jnp.bfloat16)
-        copies = exchange(lambda who: act_all.at[layer, me], act_all.at[layer], phase + 5)
+        copies = exchange(lambda who: act_all.at[layer, me], act_all.at[layer], phase + 4)
         load(layer, 5).wait()
 
-        finish(copies, act_all.at[layer], phase + 5)
+        finish(copies, act_all.at[layer], phase + 4)
         shares = []
         for who in range(n):
             packed = act_all[layer, who].astype(jnp.float32)
@@ -513,7 +544,7 @@
 
         @pl.when(layer + 1 < LAYERS)
         def _():
-            query_product(layer + 1)
+            query_product(layer + 1, True)
 
         return carry
 
@@ -569,21 +600,18 @@
             pltpu.VMEM(kv_pool.shape[:2] + kv_pool.shape[3:], bf16),
             pltpu.VMEM((LAYERS, n, LANES), f32),
             pltpu.VMEM((n, LAYERS, n, LANES), f32),
-            pltpu.VMEM((n, 16, LANES), f32),
-            pltpu.VMEM((LAYERS, n, 16, LANES), f32),
-            pltpu.VMEM((LAYERS, n, 8, LANES), f32),
+            pltpu.VMEM((LAYERS, n, PARTS, 16, q_weight.shape[2] // PARTS // 2 + LANES), bf16),
             pltpu.VMEM((8 * n, pool_dev * LANES), f32),
-            pltpu.VMEM((n, 16, LANES), f32),
-            pltpu.VMEM((LAYERS, n, 16, LANES), f32),
-            pltpu.VMEM((LAYERS, n, 8, LANES), f32),
+            pltpu.VMEM((LAYERS, n, 8 * n + 16, LANES), bf16),
             pltpu.VMEM((n, 8, 2 * WIDE + LANES), f32),
             pltpu.VMEM((LAYERS, n, 8, 2 * WIDE + LANES), f32),
             pltpu.VMEM((LAYERS, n, 16, WIDE // 2), bf16),
             pltpu.VMEM((LAYERS, 2, nt, PARTS, 16, features // PARTS // 2), bf16),
             pltpu.SemaphoreType.DMA((LAYERS, 6)),
             pltpu.SemaphoreType.DMA((n,)),
-            pltpu.SemaphoreType.DMA((6 * LAYERS + 1, n)),
+            pltpu.SemaphoreType.DMA((PHASES * LAYERS + 1, n)),
             pltpu.SemaphoreType.DMA((n,)),
+            pltpu.SemaphoreType.DMA((PARTS, n)),
             pltpu.SemaphoreType.DMA((PARTS, nt)),
             pltpu.SemaphoreType.DMA((2 * LAYERS, PARTS, nt)),
         ],
@@ -598,7 +626,7 @@
         rotary_table(head_size, position),
         block_home,
         chosen,
-        chosen_count,
+        jnp.transpose(chosen_count, (1, 2, 0)),
         q_weight,
         o_weight,
         gate_weight,

time: 75.6 us -> 65 us (0.86)
  Pallas kernels: 72.7 us -> 63.4 us
  local copies, waits for them, and re-layouts: 2.62 us -> 1.32 us
    pallas_call x1, Pallas kernels: 72.7 us -> 63.4 us  [fused_shards(): pl.pallas_call(functools.partial(decoder_kernel, n, nt), out_shape=jax.Sh...]
    unnamed x2 -> x1, local copies, waits for them, and re-layouts: 2.62 us -> 1.32 us
where the time goes in v3:
time: 65 us; the launch traced here: 64.8 us
  Pallas kernels  63.4 us (98%)
  local copies, waits for them, and re-layouts  1.32 us (2%)
    pallas_call x1, Pallas kernels, fused_shards(): pl.pallas_call(functools.partial(decoder_kernel, n, nt), out_shape=jax.Sh...  63.4 us
    unnamed x1, local copies, waits for them, and re-layouts  1.32 us

profile of v3, /device:TPU:0, one launch (start us, length us, event | category | flops | bytes accessed | tf_op | source)
XLA Modules:
  0.0 64.8 jit_solution(2306412378425561306)
XLA Ops:
  0.0 63.4 %decoder_layers.1 = bf16[8,1024]{1,0:T(8,128)(2,1)} custom-call(bf16[8,1024]{1,0:T(8,128)(2,1)} %hidden_ref.1, bf16[2,1024]{1,0:T(2,128)(2,1)} %attn_gain_ref.1, bf16[2,1024]{1,0:T(2,128)(2,1)} %ffn_gain_ref.1, f32[16,128]{1,0:T(8,128)} %constant.2.clone.turn_ref, s32[1,32]{1,0:T(1,128)} %home_ref.1, s32[2,1,1,24]{3,2,1,0:T(1,128)} %chosen_ref.1, ...), custom_call_target="tpu_custom_call" | custom-call | tf_op jit(solution)/shard_map/decoder_layers/pallas_call | solution.py:588
  63.4 1.3 %copy.15 = bf16[8,1024]{1,0:T(8,128)(2,1)} copy(bf16[8,1024]{1,0:T(8,128)(2,1)} %decoder_layers.1) | data formatting | bytes 32768

commit v4 on v3

--- a/solution.py
+++ b/solution.py
@@ -213,7 +213,7 @@
     me = lax.axis_index("req")
     my_tp = lax.axis_index("tp")
     hd = LANES
-    order = [*range(2, n), 1]
+    order = range(1, n)
     slots = kv_w.shape[1]
 
     def load(layer, which):
@@ -232,7 +232,10 @@
         return pltpu.make_async_copy(source, target.at[layer], load_sem.at[layer, which])
 
     def peer(step):
-        return lax.rem(me + step, n)
+        kind = (step - 1) // 2
+        row = (me // 4 + 1 - kind // 2) % 2
+        column = (me // 2 + 1 - kind % 2) % 2
+        return row * 4 + column * 2 + (me + step) % 2
 
     def send(source, target, step, phase):
         return pltpu.make_async_remote_copy(
@@ -261,11 +264,11 @@
         return copies
 
     def finish(copies, target, phase):
-        for step in range(1, n):
+        for copy in copies:
+            copy.wait_send()
+        for step in range(n - 1, 0, -1):
             who = peer(step)
             wait_from(target.at[who], who, phase)
-        for copy in copies:
-            copy.wait_send()
 
     def head_copy(slot, step, phase, part, who):
         return pltpu.make_async_remote_copy(
@@ -284,10 +287,12 @@
             width = product.shape[1] // 2
             packed = jnp.concatenate([product[:, :width], product[:, width:]], axis=0)
             buffer[my_tp, part] = packed.astype(jnp.bfloat16)
-            for step in range(nt - 1, 0, -1):
+            for step in range(1, nt):
                 copy = head_copy(buffer.at[my_tp, part], step, phase, part, my_tp)
                 copy.start()
                 copies.append(copy)
+        for copy in copies:
+            copy.wait_send()
         for part in range(PARTS):
             for step in range(1, nt):
                 who = lax.rem(my_tp + step, nt)
@@ -299,8 +304,6 @@
             width = total.shape[1]
             columns = slice(part * width, (part + 1) * width)
             state[:, columns] = (state[:, columns] + total).astype(jnp.bfloat16).astype(jnp.float32)
-        for copy in copies:
-            copy.wait_send()
 
     def normed(gain_ref, layer):
         current = state[...]
@@ -366,7 +369,7 @@
             used = jnp.where(slot_ids == slot, 1.0, used)
         used_out[layer] = used
     query_product(0, False)
-    for which in range(3, 6):
+    for which in (3, 4):
         load(0, which).start()
     pl.semaphore_wait(barrier, n - 1 + nt - 1)
 
@@ -401,9 +404,12 @@
         for who in range(n):
             row = jnp.where(rows8 == me, used_all[who, layer], 0.0)
             used = jnp.where(rows8 == who, jnp.sum(row, axis=0, keepdims=True), used)
+        for part in range(PARTS):
+            for copy in query_copies(layer, part):
+                copy.wait_send()
         heads = []
         for part in range(PARTS):
-            for step in range(1, n):
+            for step in range(n - 1, 0, -1):
                 who = peer(step)
                 wait_from(q_in.at[layer, who, part], who, phase + part)
             total = q_in[layer, 0, part].astype(jnp.float32)
@@ -420,10 +426,8 @@
             swapped = jnp.concatenate([query[:, hd // 2 :], query[:, : hd // 2]], axis=1)
             queries.append((query * turn_ref[0:8] + swapped * turn_ref[8:16]) * hd ** (-0.5))
         queries = jnp.concatenate(queries, axis=0).astype(jnp.bfloat16)
-        for part in range(PARTS):
-            for copy in query_copies(layer, part):
-                copy.wait_send()
-
+
+        load(layer, 5).start()
         step_slots = TOKENS // LANES
         peak = jnp.full((n * 8, LANES), MASK_FILL, jnp.float32)
         for chunk in range(slots // step_slots):
@@ -479,6 +483,11 @@
 
         width = state.shape[1] // PARTS
 
+        @pl.when(layer + 1 < LAYERS)
+        def _():
+            for which in (0, 1, 2):
+                load(layer + 1, which).start()
+
         def out_part(part):
             weight = o_w[layer, :, part * width : (part + 1) * width]
             return jnp.dot(context, weight, preferred_element_type=jnp.float32)
@@ -509,8 +518,7 @@
 
         @pl.when(layer + 1 < LAYERS)
         def _():
-            for which in range(6):
-                load(layer + 1, which).start()
+            load(layer + 1, 3).start()
 
         gate_up(me)
         ffn_in[layer, me] = ffn_out[me]
@@ -535,6 +543,10 @@
             share = jnp.concatenate([packed[0:8], packed[8:16]], axis=1)
             shares.append(share[:, (who % 2) * LANES :])
         act = jnp.concatenate(shares, axis=1).astype(jnp.bfloat16)
+
+        @pl.when(layer + 1 < LAYERS)
+        def _():
+            load(layer + 1, 4).start()
 
         def down_part(part):
             weight = down_w[layer, :, part * width : (part + 1) * width]

time: 65 us -> 63.7 us (0.980)
  Pallas kernels: 63.4 us -> 62.1 us
    pallas_call x1, Pallas kernels: 63.4 us -> 62.1 us  [fused_shards(): pl.pallas_call(functools.partial(decoder_kernel, n, nt), out_shape=jax.Sh...]
where the time goes in v4:
time: 63.7 us; the launch traced here: 63.4 us
  Pallas kernels  62.1 us (97%)
  local copies, waits for them, and re-layouts  1.32 us (2%)
    pallas_call x1, Pallas kernels, fused_shards(): pl.pallas_call(functools.partial(decoder_kernel, n, nt), out_shape=jax.Sh...  62.1 us
    unnamed x1, local copies, waits for them, and re-layouts  1.32 us

profile of v4, /device:TPU:0, one launch (start us, length us, event | category | flops | bytes accessed | tf_op | source)
XLA Modules:
  0.0 63.4 jit_solution(3266364510484372920)
XLA Ops:
  0.0 62.1 %decoder_layers.1 = bf16[8,1024]{1,0:T(8,128)(2,1)} custom-call(bf16[8,1024]{1,0:T(8,128)(2,1)} %hidden_ref.1, bf16[2,1024]{1,0:T(2,128)(2,1)} %attn_gain_ref.1, bf16[2,1024]{1,0:T(2,128)(2,1)} %ffn_gain_ref.1, f32[16,128]{1,0:T(8,128)} %constant.2.clone.turn_ref, s32[1,32]{1,0:T(1,128)} %home_ref.1, s32[2,1,1,24]{3,2,1,0:T(1,128)} %chosen_ref.1, ...), custom_call_target="tpu_custom_call" | custom-call | tf_op jit(solution)/shard_map/decoder_layers/pallas_call | solution.py:600
  62.1 1.3 %copy.15 = bf16[8,1024]{1,0:T(8,128)(2,1)} copy(bf16[8,1024]{1,0:T(8,128)(2,1)} %decoder_layers.1) | data formatting | bytes 32768

commit v5 on v4

--- a/solution.py
+++ b/solution.py
@@ -19,6 +19,7 @@
 LANES = 128
 TOKENS = 512
 WIDE = 512
+CHIP_UNITS = 896
 PARTS = 2
 PHASES = 5
 MIB = 1 << 20
@@ -312,8 +313,8 @@
         squares = jnp.sum(current * current, axis=1, keepdims=True)
         return (current * gain).astype(jnp.bfloat16), jnp.broadcast_to(squares, (current.shape[0], LANES))
 
-    def ffn_start(who):
-        return pl.multiple_of((7 * who // 2) * LANES, LANES)
+    def chip_units(chip):
+        return pl.ds(pl.multiple_of(chip * CHIP_UNITS, LANES), CHIP_UNITS)
 
     for which in range(3):
         load(0, which).start()
@@ -358,6 +359,24 @@
                 for copy in query_copies(layer, part):
                     copy.start()
 
+    query_product(0, False)
+    for which in (3, 4):
+        load(0, which).start()
+    pl.semaphore_wait(barrier, n - 1 + nt - 1)
+
+    def used_copy(step):
+        return pltpu.make_async_remote_copy(
+            src_ref=used_out,
+            dst_ref=used_all.at[me],
+            send_sem=used_sem.at[step],
+            recv_sem=recv_sem.at[PHASES * LAYERS, me],
+            device_id=(peer(step), my_tp),
+            device_id_type=MESH,
+        )
+
+    for part in range(PARTS):
+        for copy in query_copies(0, part):
+            copy.start()
     rows8 = lax.broadcasted_iota(jnp.int32, (n, LANES), 0)
     lanes8 = lax.broadcasted_iota(jnp.int32, (n, LANES), 1)
     slot_ids = jnp.where(lanes8 < slots, rows8 * slots + lanes8, -1)
@@ -368,24 +387,6 @@
             slot = jnp.where(entry < count_ref[0, 0, layer], slot, -2)
             used = jnp.where(slot_ids == slot, 1.0, used)
         used_out[layer] = used
-    query_product(0, False)
-    for which in (3, 4):
-        load(0, which).start()
-    pl.semaphore_wait(barrier, n - 1 + nt - 1)
-
-    def used_copy(step):
-        return pltpu.make_async_remote_copy(
-            src_ref=used_out,
-            dst_ref=used_all.at[me],
-            send_sem=used_sem.at[step],
-            recv_sem=recv_sem.at[PHASES * LAYERS, me],
-            device_id=(peer(step), my_tp),
-            device_id_type=MESH,
-        )
-
-    for part in range(PARTS):
-        for copy in query_copies(0, part):
-            copy.start()
     for step in order:
         used_copy(step).start()
     used_all[me] = used_out[...]
@@ -498,31 +499,34 @@
         load(layer, 3).wait()
         load(layer, 4).wait()
 
-        def gate_up(who):
-            columns = pl.ds(ffn_start(who), WIDE)
-            ffn_out[who, :, 0:WIDE] = jnp.dot(
-                scaled, gate_w[layer, :, columns], preferred_element_type=jnp.float32
-            )
-            ffn_out[who, :, WIDE : 2 * WIDE] = jnp.dot(
-                scaled, up_w[layer, :, columns], preferred_element_type=jnp.float32
-            )
-            ffn_out[who, :, 2 * WIDE :] = squares
-
-        def ffn_step(step, carry):
-            who = peer(step)
-            gate_up(who)
-            send(ffn_out.at[who], ffn_in.at[layer, me], step, phase + 3).start()
+        def gate_up(chip):
+            for index, weight in enumerate((gate_w, up_w)):
+                product = jnp.dot(scaled, weight[layer, :, chip_units(chip)], preferred_element_type=jnp.float32)
+                columns = slice(index * WIDE, (index + 1) * WIDE)
+                ffn_out[2 * chip, :, columns] = product[:, 0:WIDE]
+                ffn_out[2 * chip + 1, :, columns] = product[:, CHIP_UNITS - WIDE :]
+            ffn_out[2 * chip, :, 2 * WIDE :] = squares
+            ffn_out[2 * chip + 1, :, 2 * WIDE :] = squares
+
+        def ffn_send(step):
+            return send(ffn_out.at[peer(step)], ffn_in.at[layer, me], step, phase + 3)
+
+        def ffn_step(kind, carry):
+            gate_up(peer(2 * kind + 1) // 2)
+            ffn_send(2 * kind + 1).start()
+            ffn_send(2 * kind + 2).start()
             return carry
 
-        lax.fori_loop(1, n, ffn_step, 0)
+        lax.fori_loop(0, n // 2 - 1, ffn_step, 0)
 
         @pl.when(layer + 1 < LAYERS)
         def _():
             load(layer + 1, 3).start()
 
-        gate_up(me)
+        gate_up(me // 2)
+        ffn_send(n - 1).start()
         ffn_in[layer, me] = ffn_out[me]
-        copies = [send(ffn_out.at[peer(step)], ffn_in.at[layer, me], step, phase + 3) for step in range(1, n)]
+        copies = [ffn_send(step) for step in order]
         finish(copies, ffn_in.at[layer], phase + 3)
         total = ffn_in[layer, 0]
         for who in range(1, n):
@@ -536,21 +540,43 @@
         copies = exchange(lambda who: act_all.at[layer, me], act_all.at[layer], phase + 4)
         load(layer, 5).wait()
 
-        finish(copies, act_all.at[layer], phase + 4)
-        shares = []
-        for who in range(n):
-            packed = act_all[layer, who].astype(jnp.float32)
-            share = jnp.concatenate([packed[0:8], packed[8:16]], axis=1)
-            shares.append(share[:, (who % 2) * LANES :])
-        act = jnp.concatenate(shares, axis=1).astype(jnp.bfloat16)
+        def chip_act(chip):
+            shares = []
+            for core in range(2):
+                packed = act_all[layer, 2 * chip + core].astype(jnp.float32)
+                shares.append(jnp.concatenate([packed[0:8], packed[8:16]], axis=1))
+            both = [shares[0], shares[1][:, 2 * WIDE - CHIP_UNITS :]]
+            return jnp.concatenate(both, axis=1).astype(jnp.bfloat16)
+
+        def arrived(step):
+            wait_from(act_all.at[layer, peer(step)], peer(step), phase + 4)
+
+        arrived(n - 1)
+        sums = jnp.dot(
+            chip_act(me // 2), down_w[layer, chip_units(me // 2), :], preferred_element_type=jnp.float32
+        )
+        for copy in copies:
+            copy.wait_send()
+        for kind in range(n // 2 - 2, 0, -1):
+            arrived(2 * kind + 1)
+            arrived(2 * kind + 2)
+            chip = peer(2 * kind + 1) // 2
+            sums = sums + jnp.dot(
+                chip_act(chip), down_w[layer, chip_units(chip), :], preferred_element_type=jnp.float32
+            )
+        arrived(1)
+        arrived(2)
+        last = peer(1) // 2
+        act = chip_act(last)
 
         @pl.when(layer + 1 < LAYERS)
         def _():
             load(layer + 1, 4).start()
 
         def down_part(part):
-            weight = down_w[layer, :, part * width : (part + 1) * width]
-            return jnp.dot(act, weight, preferred_element_type=jnp.float32)
+            columns = slice(part * width, (part + 1) * width)
+            weight = down_w[layer, chip_units(last), columns]
+            return sums[:, columns] + jnp.dot(act, weight, preferred_element_type=jnp.float32)
 
         over_heads(down_part, head_sums.at[layer, 1], 2 * layer + 1)
 

time: 63.7 us -> 63.1 us (level)
  no operation moved by 1% of the time
where the time goes in v5:
time: 63.1 us; the launch traced here: 62.8 us
  Pallas kernels  61.5 us (97%)
  local copies, waits for them, and re-layouts  1.32 us (2%)
    pallas_call x1, Pallas kernels, fused_shards(): pl.pallas_call(functools.partial(decoder_kernel, n, nt), out_shape=jax.Sh...  61.5 us
    unnamed x1, local copies, waits for them, and re-layouts  1.32 us

profile of v5, /device:TPU:0, one launch (start us, length us, event | category | flops | bytes accessed | tf_op | source)
XLA Modules:
  0.0 62.8 jit_solution(7177977573667676529)
XLA Ops:
  0.0 61.5 %decoder_layers.1 = bf16[8,1024]{1,0:T(8,128)(2,1)} custom-call(bf16[8,1024]{1,0:T(8,128)(2,1)} %hidden_ref.1, bf16[2,1024]{1,0:T(2,128)(2,1)} %attn_gain_ref.1, bf16[2,1024]{1,0:T(2,128)(2,1)} %ffn_gain_ref.1, f32[16,128]{1,0:T(8,128)} %constant.2.clone.turn_ref, s32[1,32]{1,0:T(1,128)} %home_ref.1, s32[2,1,1,24]{3,2,1,0:T(1,128)} %chosen_ref.1, ...), custom_call_target="tpu_custom_call" | custom-call | tf_op jit(solution)/shard_map/decoder_layers/pallas_call | solution.py:626
  61.5 1.3 %copy.15 = bf16[8,1024]{1,0:T(8,128)(2,1)} copy(bf16[8,1024]{1,0:T(8,128)(2,1)} %decoder_layers.1) | data formatting | bytes 32768

commit v6 on v5

--- a/solution.py
+++ b/solution.py
@@ -328,11 +328,15 @@
         )
     state[...] = hidden_ref[...].astype(jnp.float32)
 
+    def query_slot(layer, who, part):
+        width = q_in.shape[4] - (LANES if part else 0)
+        return q_in.at[layer, who, part, :, 0:width]
+
     def query_copies(layer, part):
         return [
             pltpu.make_async_remote_copy(
-                src_ref=q_in.at[layer, me, part],
-                dst_ref=q_in.at[layer, me, part],
+                src_ref=query_slot(layer, me, part),
+                dst_ref=query_slot(layer, me, part),
                 send_sem=q_send_sem.at[part, step],
                 recv_sem=recv_sem.at[PHASES * layer + part, me],
                 device_id=(peer(step), my_tp),
@@ -412,13 +416,14 @@
         for part in range(PARTS):
             for step in range(n - 1, 0, -1):
                 who = peer(step)
-                wait_from(q_in.at[layer, who, part], who, phase + part)
-            total = q_in[layer, 0, part].astype(jnp.float32)
+                wait_from(query_slot(layer, who, part), who, phase + part)
+            total = query_slot(layer, 0, part)[...].astype(jnp.float32)
             for who in range(1, n):
-                total = total + q_in[layer, who, part].astype(jnp.float32)
-            width = total.shape[1] - LANES
-            squares = total[0:8, width:] + total[8:16, width:]
-            inv = lax.rsqrt(squares / D + EPSILON)
+                total = total + query_slot(layer, who, part)[...].astype(jnp.float32)
+            width = q_in.shape[4] - LANES
+            if part == 0:
+                squares = total[0:8, width:] + total[8:16, width:]
+                inv = lax.rsqrt(squares / D + EPSILON)
             for half in range(2):
                 for head in range(width // hd):
                     heads.append(total[half * 8 : half * 8 + 8, head * hd : (head + 1) * hd] * inv)

time: 63.1 us -> 62.6 us (level)
  no operation moved by 1% of the time
where the time goes in v6:
time: 62.6 us; the launch traced here: 62.3 us
  Pallas kernels  61 us (97%)
  local copies, waits for them, and re-layouts  1.32 us (2%)
    pallas_call x1, Pallas kernels, fused_shards(): pl.pallas_call(functools.partial(decoder_kernel, n, nt), out_shape=jax.Sh...  61 us
    unnamed x1, local copies, waits for them, and re-layouts  1.32 us

profile of v6, /device:TPU:0, one launch (start us, length us, event | category | flops | bytes accessed | tf_op | source)
XLA Modules:
  0.0 62.3 jit_solution(16316142956566939526)
XLA Ops:
  0.0 61.0 %decoder_layers.1 = bf16[8,1024]{1,0:T(8,128)(2,1)} custom-call(bf16[8,1024]{1,0:T(8,128)(2,1)} %hidden_ref.1, bf16[2,1024]{1,0:T(2,128)(2,1)} %attn_gain_ref.1, bf16[2,1024]{1,0:T(2,128)(2,1)} %ffn_gain_ref.1, f32[16,128]{1,0:T(8,128)} %constant.2.clone.turn_ref, s32[1,32]{1,0:T(1,128)} %home_ref.1, s32[2,1,1,24]{3,2,1,0:T(1,128)} %chosen_ref.1, ...), custom_call_target="tpu_custom_call" | custom-call | tf_op jit(solution)/shard_map/decoder_layers/pallas_call | solution.py:631
  61.0 1.3 %copy.15 = bf16[8,1024]{1,0:T(8,128)(2,1)} copy(bf16[8,1024]{1,0:T(8,128)(2,1)} %decoder_layers.1) | data formatting | bytes 32768
